TPU v7x, 32 devices: a whole 2x2x4 slice. The times are simulated.
32 devices in a mesh: dp: 4 (over y, x), row: 2 (over core), col: 4 (over z).
Axes of the slice: x: 2, y: 2, z: 4, core: 2. Of those that a mesh axis runs over, the one named last changes fastest.
Arguments:
- tokens: bfloat16 [64, 196, 1280], P(('dp', 'row', 'col')), may hold values from -72 to 72
- valid_mask: int32 [64, 196], P(('dp', 'row', 'col')), may hold values from 0 to 1, as said below
- out_grad: bfloat16 [64, 196, 1280], P(('dp', 'row', 'col')), may hold values from -6 to 6
- first_gain: float32 [1280], replicated, may hold values from 0.5 to 1.5
- first_shift: float32 [1280], replicated, may hold values from -1 to 1
- qkv_weight: bfloat16 [1280, 3, 1280], P('row', None, 'col'), may hold values from -1 to 1
- qkv_bias: float32 [2, 1280], P(None, 'col'), may hold values from -1 to 1
- rel_height: float32 [27, 80], replicated, may hold values from -0.9 to 0.9
- rel_width: float32 [27, 80], replicated, may hold values from -0.9 to 0.9
- proj_weight: bfloat16 [1280, 1280], P('col', 'row'), may hold values from -0.625 to 0.625
- proj_bias: float32 [1280], replicated, may hold values from -1 to 1
- second_gain: float32 [1280], replicated, may hold values from 0.5 to 1.5
- second_shift: float32 [1280], replicated, may hold values from -1 to 1
- expand_weight: bfloat16 [1280, 5120], P('row', 'col'), may hold values from -1 to 1
- expand_bias: float32 [5120], P('col'), may hold values from -1 to 1
- shrink_weight: bfloat16 [5120, 1280], P('col', 'row'), may hold values from -0.078125 to 0.078125
- shrink_bias: float32 [1280], replicated, may hold values from -1 to 1
Outputs:
- block_out: bfloat16 [64, 196, 1280], P(('dp', 'row', 'col'))
- input_grad: float32 [64, 196, 1280], P(('dp', 'row', 'col'))
- first_gain_grad: float32 [1280], replicated
- first_shift_grad: float32 [1280], replicated
- qkv_weight_grad: float32 [1280, 3, 1280], P('row', None, 'col')
- qkv_bias_grad: float32 [2, 1280], P(None, 'col')
- rel_height_grad: float32 [27, 80], replicated
- rel_width_grad: float32 [27, 80], replicated
- proj_weight_grad: float32 [1280, 1280], P('col', 'row')
- proj_bias_grad: float32 [1280], replicated
- second_gain_grad: float32 [1280], replicated
- second_shift_grad: float32 [1280], replicated
- expand_weight_grad: float32 [1280, 5120], P('row', 'col')
- expand_bias_grad: float32 [5120], P('col')
- shrink_weight_grad: float32 [5120, 1280], P('col', 'row')
- shrink_bias_grad: float32 [1280], replicated
- rms: float32 [5], replicated
Inputs may be any that keep to these rules, and one draw needn't show every extreme that they name: `valid_mask`: windows come 25 to an image, 5 by 5 windows of 14 by 14 tokens in row-major order, the last image possibly incomplete; 1 marks tokens inside the image content, a rectangle at the top left that is 64 tokens along one side and at least half of that along the other.
All inputs are finite; a program needn't handle non-finite values.
Results may differ from a plain program's by a relative error of at most 0.012.
Values may be sent and summed in bfloat16 or wider, within the bound.
A program may use at most 256 MiB of HBM per device.

v0:
```python
import jax
import jax.numpy as jnp
from jax import lax
from jax.sharding import PartitionSpec as P

epsilon = 1e-06
highest = lax.Precision.HIGHEST


def layer_norm(values, norm_gain, norm_shift):
    center = values - jnp.mean(values, axis=-1, keepdims=True)
    spread = jnp.mean(center * center, axis=-1, keepdims=True)
    return center * lax.rsqrt(spread + epsilon) * norm_gain + norm_shift


def offset_table(span_size):
    positions = jnp.arange(span_size)
    offset = positions[:, None] - positions[None, :] + span_size - 1
    return (offset[:, :, None] == jnp.arange(2 * span_size - 1)[None, None, :]).astype(jnp.float32)


def attention_scores(
    query_rows, key_rows, rel_rows_table, rel_cols_table, onehot_table, span_size, scaling
):
    window_count, tokens_per, head_count, head_size = query_rows.shape
    rel_count = 2 * span_size - 1
    direct = (
        jnp.einsum("bthc,buhc->bhtu", query_rows, key_rows, preferred_element_type=jnp.float32)
        * scaling
    )
    query_float = query_rows.astype(jnp.float32)
    along_rows = jnp.einsum("bthc,jc->bhtj", query_float, rel_rows_table, precision=highest)
    along_cols = jnp.einsum("bthc,jc->bhtj", query_float, rel_cols_table, precision=highest)
    grid_rows = along_rows.reshape(window_count, head_count, span_size, span_size, rel_count)
    grid_cols = along_cols.reshape(window_count, head_count, span_size, span_size, rel_count)
    rel_rows = jnp.einsum("bhxyj,xkj->bhxyk", grid_rows, onehot_table, precision=highest)
    rel_cols = jnp.einsum("bhxyj,ywj->bhxyw", grid_cols, onehot_table, precision=highest)
    score_sum = direct.reshape(window_count, head_count, span_size, span_size, span_size, span_size)
    score_sum = score_sum + rel_rows[:, :, :, :, :, None] + rel_cols[:, :, :, :, None, :]
    return score_sum.reshape(window_count, head_count, tokens_per, tokens_per)


def relative_back(score_float, onehot_table, span_size):
    window_count, head_count, tokens_per, other_tokens = score_float.shape
    grid = score_float.reshape(window_count, head_count, span_size, span_size, span_size, span_size)
    rows_part = jnp.einsum("bhxykw,xkj->bhxyj", grid, onehot_table, precision=highest)
    cols_part = jnp.einsum("bhxykw,ywj->bhxyj", grid, onehot_table, precision=highest)
    return (
        rows_part.reshape(window_count, head_count, tokens_per, -1),
        cols_part.reshape(window_count, head_count, tokens_per, -1),
    )


def gather_weights(qkv_weight, proj_weight, expand_weight, shrink_weight):
    return (
        lax.all_gather(qkv_weight, "row", axis=0, tiled=True),
        lax.all_gather(proj_weight, "row", axis=1, tiled=True),
        lax.all_gather(expand_weight, "row", axis=0, tiled=True),
        lax.all_gather(shrink_weight, "row", axis=1, tiled=True),
    )


def gather_tokens(normed):
    return lax.all_gather(normed, "col", axis=0, tiled=True)


def gather_grads(grad_low):
    return lax.all_gather(grad_low, "col", axis=0, tiled=True)


def sum_branch(inputs_low, weight_full, own_windows):

    def term(first_row, row_count):
        return jnp.einsum(
            "btk,kd->btd", inputs_low, weight_full, preferred_element_type=jnp.float32
        )

    return lax.psum_scatter(
        term(jnp.int32(0), own_windows * lax.axis_size("col")),
        "col",
        scatter_dimension=0,
        tiled=True,
    )


def sum_input(grads_low, weight_full, own_windows):

    def term(first_row, row_count):
        return jnp.einsum("btk,dk->btd", grads_low, weight_full, preferred_element_type=jnp.float32)

    return lax.psum_scatter(
        term(jnp.int32(0), own_windows * lax.axis_size("col")),
        "col",
        scatter_dimension=0,
        tiled=True,
    )


def activate(values):
    return jax.nn.gelu(values, approximate=False)


def per_device(
    tokens,
    valid_mask,
    out_grad,
    first_gain,
    first_shift,
    qkv_weight,
    qkv_bias,
    rel_height,
    rel_width,
    proj_weight,
    proj_bias,
    second_gain,
    second_shift,
    expand_weight,
    expand_bias,
    shrink_weight,
    shrink_bias,
):
    span_size = (rel_height.shape[0] + 1) // 2
    head_size = rel_height.shape[1]
    local_width = qkv_weight.shape[2]
    head_count = local_width // head_size
    own_windows = tokens.shape[0]
    tokens_per = tokens.shape[1]
    model_width = tokens.shape[2]
    scaling = head_size ** (-0.5)
    onehot_table = offset_table(span_size)
    inputs = tokens.astype(jnp.float32)
    keep_mask = valid_mask.astype(jnp.float32)[:, :, None]

    def first_norm(values, norm_gain, norm_shift):
        return layer_norm(values, norm_gain, norm_shift) * keep_mask

    qkv_full, proj_full, expand_full, shrink_full = gather_weights(
        qkv_weight, proj_weight, expand_weight, shrink_weight
    )
    normed_first, first_back = jax.vjp(first_norm, inputs, first_gain, first_shift)
    first_all = gather_tokens(normed_first.astype(jnp.bfloat16))
    all_windows = first_all.shape[0]
    bias_rows = jnp.stack([qkv_bias[0], jnp.zeros_like(qkv_bias[0]), qkv_bias[1]])
    projected = (
        jnp.einsum("btd,dsk->btsk", first_all, qkv_full, preferred_element_type=jnp.float32)
        + bias_rows
    )
    projected = projected.astype(jnp.bfloat16)
    head_shape = (all_windows, tokens_per, head_count, head_size)
    query_low = projected[:, :, 0].reshape(head_shape)
    key_low = projected[:, :, 1].reshape(head_shape)
    value_low = projected[:, :, 2].reshape(head_shape)
    scores = attention_scores(
        query_low, key_low, rel_height, rel_width, onehot_table, span_size, scaling
    )
    top_score = jnp.max(scores, axis=-1, keepdims=True)
    log_total = top_score + jnp.log(jnp.sum(jnp.exp(scores - top_score), axis=-1, keepdims=True))
    probs_low = jnp.exp(scores - log_total).astype(jnp.bfloat16)
    attended = jnp.einsum(
        "bhtu,buhc->bthc", probs_low, value_low, preferred_element_type=jnp.float32
    )
    attended_low = attended.reshape(all_windows, tokens_per, local_width).astype(jnp.bfloat16)
    attn_out = sum_branch(attended_low, proj_full, own_windows) + proj_bias
    middle = inputs + attn_out
    normed_second, second_back = jax.vjp(layer_norm, middle, second_gain, second_shift)
    second_all = gather_tokens(normed_second.astype(jnp.bfloat16))
    hidden_pre = (
        jnp.einsum("btd,df->btf", second_all, expand_full, preferred_element_type=jnp.float32)
        + expand_bias
    )
    active_value, active_back = jax.vjp(activate, hidden_pre)
    hidden_low = active_value.astype(jnp.bfloat16)
    mlp_out = sum_branch(hidden_low, shrink_full, own_windows) + shrink_bias
    result = middle + mlp_out
    stat_terms = jnp.stack(
        [
            jnp.sum(keep_mask * inputs * inputs),
            jnp.sum(keep_mask * middle * middle),
            jnp.sum(keep_mask * result * result),
            jnp.sum(keep_mask * attn_out * attn_out),
            jnp.sum(keep_mask * mlp_out * mlp_out),
        ]
    )
    valid_count = jnp.sum(keep_mask)
    stat_total, count_total = lax.psum((stat_terms, valid_count), ("dp", "row", "col"))
    out_float = out_grad.astype(jnp.float32)
    qkv_full, proj_full, expand_full, shrink_full = gather_weights(
        qkv_weight, proj_weight, expand_weight, shrink_weight
    )
    mlp_grad_low = out_float.astype(jnp.bfloat16)
    shrink_bias_grad = jnp.sum(mlp_grad_low, axis=(0, 1), dtype=jnp.float32)
    mlp_grad_all = gather_grads(mlp_grad_low)
    shrink_grad_full = jnp.einsum(
        "btf,btd->fd", hidden_low, mlp_grad_all, preferred_element_type=jnp.float32
    )
    hidden_grad = jnp.einsum(
        "btd,fd->btf", mlp_grad_all, shrink_full, preferred_element_type=jnp.float32
    )
    pre_grad_low = active_back(hidden_grad)[0].astype(jnp.bfloat16)
    expand_bias_grad = jnp.sum(pre_grad_low, axis=(0, 1), dtype=jnp.float32)
    expand_grad_full = jnp.einsum(
        "btd,btf->df", second_all, pre_grad_low, preferred_element_type=jnp.float32
    )
    second_grad = sum_input(pre_grad_low, expand_full, own_windows)
    middle_part, second_gain_grad, second_shift_grad = second_back(second_grad)
    middle_grad = out_float + middle_part
    attn_grad_low = middle_grad.astype(jnp.bfloat16)
    proj_bias_grad = jnp.sum(attn_grad_low, axis=(0, 1), dtype=jnp.float32)
    attn_grad_all = gather_grads(attn_grad_low)
    proj_grad_full = jnp.einsum(
        "btk,btd->kd", attended_low, attn_grad_all, preferred_element_type=jnp.float32
    )
    attended_grad = jnp.einsum(
        "btd,kd->btk", attn_grad_all, proj_full, preferred_element_type=jnp.float32
    )
    attended_grad = attended_grad.astype(jnp.bfloat16).reshape(head_shape)
    scores_again = attention_scores(
        query_low, key_low, rel_height, rel_width, onehot_table, span_size, scaling
    )
    probs_float = jnp.exp(scores_again - log_total)
    probs_again = probs_float.astype(jnp.bfloat16)
    prob_grad = jnp.einsum(
        "bthc,buhc->bhtu", attended_grad, value_low, preferred_element_type=jnp.float32
    )
    value_grad = jnp.einsum(
        "bhtu,bthc->buhc", probs_again, attended_grad, preferred_element_type=jnp.float32
    )
    score_grad = probs_float * (
        prob_grad - jnp.sum(probs_float * prob_grad, axis=-1, keepdims=True)
    )
    score_low = score_grad.astype(jnp.bfloat16)
    rows_grad, cols_grad = relative_back(score_low.astype(jnp.float32), onehot_table, span_size)
    query_float = query_low.astype(jnp.float32)
    query_grad = (
        jnp.einsum("bhtu,buhc->bthc", score_low, key_low, preferred_element_type=jnp.float32)
        * scaling
    )
    query_grad = query_grad + jnp.einsum("bhtj,jc->bthc", rows_grad, rel_height, precision=highest)
    query_grad = query_grad + jnp.einsum("bhtj,jc->bthc", cols_grad, rel_width, precision=highest)
    key_grad = (
        jnp.einsum("bhtu,bthc->buhc", score_low, query_low, preferred_element_type=jnp.float32)
        * scaling
    )
    rel_height_grad = jnp.einsum("bhtj,bthc->jc", rows_grad, query_float, precision=highest)
    rel_width_grad = jnp.einsum("bhtj,bthc->jc", cols_grad, query_float, precision=highest)
    flat_shape = (all_windows, tokens_per, local_width)
    qkv_grad_low = jnp.stack(
        [
            query_grad.reshape(flat_shape),
            key_grad.reshape(flat_shape),
            value_grad.reshape(flat_shape),
        ],
        axis=2,
    ).astype(jnp.bfloat16)
    qkv_bias_grad = jnp.sum(qkv_grad_low[:, :, 0::2], axis=(0, 1), dtype=jnp.float32)
    qkv_grad_full = jnp.einsum(
        "btd,btsk->dsk", first_all, qkv_grad_low, preferred_element_type=jnp.float32
    )
    first_grad = sum_input(
        qkv_grad_low.reshape(all_windows, tokens_per, 3 * local_width),
        qkv_full.reshape(qkv_full.shape[0], 3 * local_width),
        own_windows,
    )
    input_part, first_gain_grad, first_shift_grad = first_back(first_grad)
    input_grad = middle_grad + input_part
    qkv_rows, proj_rows, expand_rows, shrink_rows = (
        lax.psum_scatter(qkv_grad_full, "row", scatter_dimension=0, tiled=True),
        lax.psum_scatter(proj_grad_full, "row", scatter_dimension=1, tiled=True),
        lax.psum_scatter(expand_grad_full, "row", scatter_dimension=0, tiled=True),
        lax.psum_scatter(shrink_grad_full, "row", scatter_dimension=1, tiled=True),
    )
    qkv_sum, proj_sum, expand_sum, shrink_sum = lax.psum(
        (qkv_rows, proj_rows, expand_rows, shrink_rows), "dp"
    )
    qkv_bias_sum, expand_bias_sum = lax.psum((qkv_bias_grad, expand_bias_grad), ("dp", "row"))
    (
        gain_one_sum,
        shift_one_sum,
        gain_two_sum,
        shift_two_sum,
        proj_bias_sum,
        shrink_bias_sum,
        height_sum,
        width_sum,
    ) = lax.psum(
        (
            first_gain_grad,
            first_shift_grad,
            second_gain_grad,
            second_shift_grad,
            proj_bias_grad,
            shrink_bias_grad,
            rel_height_grad,
            rel_width_grad,
        ),
        ("dp", "row", "col"),
    )
    rms = jnp.sqrt(stat_total / (count_total * model_width))
    return (
        result.astype(jnp.bfloat16),
        input_grad,
        gain_one_sum,
        shift_one_sum,
        qkv_sum,
        qkv_bias_sum,
        height_sum,
        width_sum,
        proj_sum,
        proj_bias_sum,
        gain_two_sum,
        shift_two_sum,
        expand_sum,
        expand_bias_sum,
        shrink_sum,
        shrink_bias_sum,
        rms,
    )


def solution(mesh):
    in_specs = (
        P(("dp", "row", "col"), None, None),
        P(("dp", "row", "col"), None),
        P(("dp", "row", "col"), None, None),
        P(),
        P(),
        P("row", None, "col"),
        P(None, "col"),
        P(),
        P(),
        P("col", "row"),
        P(),
        P(),
        P(),
        P("row", "col"),
        P("col"),
        P("col", "row"),
        P(),
    )
    out_specs = (
        P(("dp", "row", "col"), None, None),
        P(("dp", "row", "col"), None, None),
        P(),
        P(),
        P("row", None, "col"),
        P(None, "col"),
        P(),
        P(),
        P("col", "row"),
        P(),
        P(),
        P(),
        P("row", "col"),
        P("col"),
        P("col", "row"),
        P(),
        P(),
    )
    return jax.shard_map(
        per_device, mesh=mesh, in_specs=in_specs, out_specs=out_specs, check_vma=False
    )
```

profile of v0, /device:TPU:0, one launch (start us, length us, event | category | flops | bytes accessed | tf_op | source)
XLA Modules:
  0.0 1564.0 jit_solution(9779695611453468725)
XLA Ops:
  16.8 6.6 all-gather.10.cloned.1.call-done
  23.4 82.5 %all-gather.8.cloned.1.call-done = bf16[8,196,1280]{2,1,0:T(8,128)(2,1)} async-done(((bf16[2,196,1280]{2,1,0:T(8,128)(2,1)}), bf16[8,196,1280]{2,1,0:T(8,128)(2,1)}) %all-gather.8.cloned.1.call-update) | async-done | bytes 4014096 | tf_op jit(solution)/shard_map/all_gather | solution.py:64
  105.9 8.1 add_convert_fusion.1
  128.3 16.6 %fusion.51 = f32[8,4,14,14,14]{3,4,1,0,2:T(8,128)} fusion(f32[8,4,14,14,27]{4,0,3,2,1:T(8,128)} %bitcast.176, s32[14,14]{1,0:T(8,128)S(1)} %subtract_add_fusion), kind=kOutput, calls=%fused_computation.98 | convolution fusion | flops 28455084 | bytes 1029392 | tf_op jit(solution)/shard_map/bhxyj,xkj->bhxyk/dot_general | solution.py:36
  144.9 6.2 copy.105
  151.1 3.7 copy.107
  154.8 16.6 %fusion.54 = f32[8,4,14,14,14]{2,4,1,0,3:T(8,128)} fusion(f32[8,4,14,14,27]{4,0,3,2,1:T(8,128)} %bitcast.177, s32[14,14]{1,0:T(8,128)S(1)} %subtract_add_fusion), kind=kOutput, calls=%fused_computation.99 | convolution fusion | flops 28455084 | bytes 1029392 | tf_op jit(solution)/shard_map/bhxyj,ywj->bhxyw/dot_general | solution.py:37
  171.4 6.2 copy.109
  177.6 17.8 %add.190 = f32[8,4,14,14,14,14]{5,4,0,3,2,1:T(8,128)} broadcast(f32[8,4,14,14,14]{4,0,3,2,1:T(8,128)} %copy.109), dimensions={0,1,2,3,5} | broadcast | bytes 5268480 | tf_op jit(solution)/shard_map/add | solution.py:39
  195.4 35.8 %add.191 = f32[8,4,196,196]{3,0,2,1:T(8,128)} reshape(f32[8,4,14,14,14,14]{5,4,0,3,2,1:T(8,128)} %add.190) | data formatting | bytes 9834496 | tf_op jit(solution)/shard_map/add | solution.py:39
  231.2 9.0 copy.110
  240.2 19.1 %add.187 = f32[8,4,14,14,14,14]{5,4,0,3,2,1:T(8,128)} broadcast(f32[8,4,14,14,14]{4,0,3,2,1:T(8,128)} %copy.105), dimensions={0,1,2,3,4} | broadcast | bytes 5268480 | tf_op jit(solution)/shard_map/add | solution.py:39
  259.3 35.8 %add.188 = f32[8,4,196,196]{3,0,2,1:T(8,128)} reshape(f32[8,4,14,14,14,14]{5,4,0,3,2,1:T(8,128)} %add.187) | data formatting | bytes 9834496 | tf_op jit(solution)/shard_map/add | solution.py:39
  295.1 9.4 copy.106
  304.5 6.6 fusion.95
  316.2 5.5 fusion.67
  322.4 139.4 %reduce-scatter.9.cloned.1.call-done = f32[2,196,1280]{2,1,0:T(8,128)} async-done(((f32[8,196,1280]{2,1,0:T(8,128)}), f32[2,196,1280]{2,1,0:T(8,128)}) %reduce-scatter.9.cloned.1.call-update) | async-done | bytes 2007056 | tf_op jit(solution)/shard_map/reduce_scatter | solution.py:78
  467.3 9.0 all-gather.14.cloned.1.call-done
  476.3 82.4 %all-gather.12.cloned.1.call-done = bf16[8,196,1280]{2,1,0:T(8,128)(2,1)} async-done(((bf16[2,196,1280]{2,1,0:T(8,128)(2,1)}), bf16[8,196,1280]{2,1,0:T(8,128)(2,1)}) %all-gather.12.cloned.1.call-update) | async-done | bytes 4014096 | tf_op jit(solution)/shard_map/all_gather | solution.py:64
  558.7 11.0 fusion.50
  572.9 19.7 %multiply_convert_fusion = (bf16[8,196,1280]{2,1,0:T(8,128)(2,1)}, f32[8,196,1280]{2,1,0:T(8,128)}) fusion(f32[8,196,1280]{2,1,0:T(8,128)S(1)} %get-tuple-element.118, f32[1280]{0:T(1024)S(1)} %copy-done.42, u8[196,1280]{1,0:T(8,128)(4,1)S(1)} %get-tuple-element.71, u8[196,1280]{1,0:T(8,128)(4,1)S(1)} %get-tuple-element.70), kind=kLoop, calls=%fused_computation.11 | loop fusion | flops 142499840 | bytes 20577280 | tf_op jit(solution)/shard_map/convert_element_type | solution.py:172
  592.6 61.0 %all-gather.18.cloned.1.call-done = bf16[8,196,1280]{2,1,0:T(8,128)(2,1)} async-done(((bf16[2,196,1280]{2,1,0:T(8,128)(2,1)}), bf16[8,196,1280]{2,1,0:T(8,128)(2,1)}) %all-gather.18.cloned.1.call-update) | async-done | bytes 4014096 | tf_op jit(solution)/shard_map/all_gather | solution.py:68
  653.6 14.2 convert_reduce_fusion
  669.8 7.7 fusion.21
  677.5 10.3 fusion.19
  687.9 129.6 %reduce-scatter.13.cloned.1.call-done = f32[2,196,1280]{2,1,0:T(8,128)} async-done(((f32[8,196,1280]{2,1,0:T(8,128)}), f32[2,196,1280]{2,1,0:T(8,128)}) %reduce-scatter.13.cloned.1.call-update) | async-done | bytes 2007056 | tf_op jit(solution)/shard_map/reduce_scatter | solution.py:91
  817.5 144.4 %reduce-scatter.11.cloned.1.call-done = f32[2,196,1280]{2,1,0:T(8,128)} async-done(((f32[8,196,1280]{2,1,0:T(8,128)}), f32[2,196,1280]{2,1,0:T(8,128)}) %reduce-scatter.11.cloned.1.call-update) | async-done | bytes 2007056 | tf_op jit(solution)/shard_map/reduce_scatter | solution.py:78
  962.0 5.2 fusion.45
  970.6 10.9 convolution_bitcast_fusion.1
  981.5 11.0 convolution_bitcast_fusion
  993.0 57.5 %all-gather.20.cloned.1.call-done = bf16[8,196,1280]{2,1,0:T(8,128)(2,1)} async-done(((bf16[2,196,1280]{2,1,0:T(8,128)(2,1)}), bf16[8,196,1280]{2,1,0:T(8,128)(2,1)}) %all-gather.20.cloned.1.call-update) | async-done | bytes 4014096 | tf_op jit(solution)/shard_map/all_gather | solution.py:68
  1050.5 4.5 convolution_convert_fusion.2
  1055.7 6.6 convolution_convert_fusion
  1065.1 5.7 multiply_reduce_fusion
  1074.1 8.0 copy.117
  1082.2 33.3 %reshape.169 = f32[8,4,14,14,14,14]{5,4,0,3,2,1:T(8,128)} reshape(f32[8,4,196,196]{3,0,2,1:T(8,128)} %copy.117) | data formatting | bytes 9834496 | tf_op jit(solution)/shard_map/reshape | solution.py:45
  1115.5 5.0 convolution_bitcast_fusion.4
  1120.6 20.2 %fusion.88 = (f32[8,4,14,14,14]{4,0,3,2,1:T(8,128)}, f32[8,4,14,14,14]{4,0,3,2,1:T(8,128)}) fusion(f32[8,4,14,14,14,14]{5,4,0,3,2,1:T(8,128)} %reshape.169), kind=kLoop, calls=%fused_computation.144 | loop fusion | flops 2283008 | bytes 5619712 | tf_op jit(solution)/shard_map/bhxykw,xkj->bhxyj/reduce_sum | solution.py:46
  1145.7 4.3 fusion.57
  1156.3 4.7 fusion.60
  1164.5 3.7 copy.123
  1178.5 10.1 convolution_bitcast_fusion.3
  1188.9 11.0 convolution_bitcast_fusion.2
  1207.3 24.7 %all-reduce.1 = (f32[2,320]{1,0:T(2,128)}, f32[1280]{0:T(1024)}) all-reduce(f32[2,320]{1,0:T(2,128)S(1)} %convert_reduce_fusion.1, f32[1280]{0:T(1024)S(1)} %get-tuple-element.121), channel_id=1, replica_groups=mesh['dp'=4,'row'=2,'col'=4] {'dp','row'}, use_global_device_ids=true, to_apply=%region_24.0 | all-reduce | flops 1920 | bytes 15360 | tf_op jit(solution)/shard_map/psum | solution.py:275
  1235.5 109.3 %reduce-scatter.15.cloned.1.call-done = f32[2,196,1280]{2,1,0:T(8,128)} async-done(((f32[8,196,1280]{2,1,0:T(8,128)}), f32[2,196,1280]{2,1,0:T(8,128)}) %reduce-scatter.15.cloned.1.call-update) | async-done | bytes 2007056 | tf_op jit(solution)/shard_map/reduce_scatter | solution.py:91
  1347.1 3.9 fusion.41
  1357.8 43.4 %all-reduce = (f32[1280]{0:T(1024)}, f32[1280]{0:T(1024)}, f32[27,80]{1,0:T(8,128)}, f32[27,80]{1,0:T(8,128)}, f32[1280]{0:T(1024)}, /*index=5*/f32[1280]{0:T(10...) all-reduce(f32[1280]{0:T(1024)S(1)} %get-tuple-element.74, ...), channel_id=1, replica_groups=mesh['dp'=4,'row'=2,'col'=4] {'dp','row','col'}, use_global_device_ids=true, to_apply=%region_18.0 | all-reduce | flops 12006 | bytes 96048 | tf_op jit(solution)/shard_map/psum | solution.py:285
  1402.4 145.4 %all-reduce.5.cloned.1.call-done = (f32[640,3,320]{0,2,1:T(8,128)}, f32[320,640]{1,0:T(8,128)}, f32[640,1280]{1,0:T(8,128)}, f32[1280,640]{1,0:T(8,128)}) async-done(((f32[640,3,320]{0,2,1:T(8,128)}, f32[320,640]{1,0:T(8,128)}, f32[640,1280]{1,0:T(8,128)}, f32[1280,640]{1,0:T(8,128)}), (f32[640,3,320]{0,2,1:T(8,128)}, f32[320,640]{1,0:T(8,128)}, f32[640,1280]{1,0:T(8,128)}, ...) | async-done | bytes 9830416 | tf_op jit(solution)/shard_map/psum | solution.py:272
  (198 shorter events, 105.7 us)
Async XLA Ops:
  7.2 111.8 %copy-start = (f32[27,80]{1,0:T(8,128)S(1)}, f32[27,80]{1,0:T(8,128)}, u32[]{:S(2)}) copy-start(f32[27,80]{1,0:T(8,128)} %param.25) | copy-start | bytes 25924
  7.2 6.9 copy-start.24
  7.2 16.2 %all-gather.10.cloned.1.call-start = ((), (), s32[]{:S(2)}) async-start(), calls=%async_computation.9 | async-start | bytes 3686400 | tf_op jit(solution)/shard_map/all_gather | solution.py:56
  8.0 8.8 copy-start.45
  8.0 97.9 %all-gather.8.cloned.1.call-start = ((), (), s32[]{:S(2)}) async-start(), calls=%async_computation.8 | async-start | bytes 5120000 | tf_op jit(solution)/shard_map/all_gather | solution.py:64
  8.7 97.2 %copy-start.31 = (f32[2,196]{1,0:T(2,128)}, f32[2,196]{1,0:T(2,128)S(1)}, u32[]{:S(2)}) copy-start(f32[2,196]{1,0:T(2,128)S(1)} %convert_element_type.67) | copy-start | bytes 4708
  10.1 95.8 %copy-start.28 = (f32[2,196]{1,0:T(2,128)}, f32[2,196]{1,0:T(2,128)S(1)}, u32[]{:S(2)}) copy-start(f32[2,196]{1,0:T(2,128)S(1)} %broadcast_multiply_fusion.1) | copy-start | bytes 4708
  11.8 94.1 %copy-start.39 = (f32[2,196]{1,0:T(2,128)}, f32[2,196]{1,0:T(2,128)S(1)}, u32[]{:S(2)}) copy-start(f32[2,196]{1,0:T(2,128)S(1)} %fusion.46) | copy-start | bytes 4708
  11.8 94.1 %copy-start.37 = (f32[2,196]{1,0:T(2,128)}, f32[2,196]{1,0:T(2,128)S(1)}, u32[]{:S(2)}) copy-start(f32[2,196]{1,0:T(2,128)S(1)} %fusion.86) | copy-start | bytes 4708
  14.0 447.8 %reduce-scatter.9.cloned.1.call-start = ((), (), s32[]{:S(2)}) async-start(), calls=%async_computation.10 | async-start | bytes 10240000 | tf_op jit(solution)/shard_map/reduce_scatter | solution.py:78
  14.2 140.6 %copy-start.25 = (s32[14,14]{1,0:T(8,128)}, s32[14,14]{1,0:T(8,128)S(1)}, u32[]{:S(2)}) copy-start(s32[14,14]{1,0:T(8,128)S(1)} %subtract_add_fusion) | copy-start | bytes 2356
  119.0 185.5 %copy-start.2 = (bf16[8,196,1,320]{1,3,0,2:T(8,128)(2,1)}, bf16[8,196,1,320]{1,3,0,2:T(8,128)(2,1)S(1)}, u32[]{:S(2)}) copy-start(bf16[8,196,1,320]{1,3,0,2:T(8,128)(2,1)S(1)} %copy.101) | copy-start | bytes 3010564
  321.7 140.1 %copy-start.35 = (f32[1280]{0:T(1024)S(1)}, f32[1280]{0:T(1024)}, u32[]{:S(2)}) copy-start(f32[1280]{0:T(1024)} %param.27) | copy-start | bytes 15364
  321.7 154.6 %all-gather.14.cloned.1.call-start = ((), (), s32[]{:S(2)}) async-start(), calls=%async_computation.12 | async-start | bytes 4915200 | tf_op jit(solution)/shard_map/all_gather | solution.py:58
  322.3 141.8 %copy-start.30 = (f32[1280]{0:T(1024)S(1)}, f32[1280]{0:T(1024)}, u32[]{:S(2)}) copy-start(f32[1280]{0:T(1024)} %param.28) | copy-start | bytes 15364
  322.3 141.8 %copy-start.41 = (f32[1280]{0:T(1024)S(1)}, f32[1280]{0:T(1024)}, u32[]{:S(2)}) copy-start(f32[1280]{0:T(1024)} %param.29) | copy-start | bytes 15364
  322.3 236.4 %all-gather.12.cloned.1.call-start = ((), (), s32[]{:S(2)}) async-start(), calls=%async_computation.11 | async-start | bytes 5120000 | tf_op jit(solution)/shard_map/all_gather | solution.py:64
  465.5 93.2 %copy-start.42 = (f32[1280]{0:T(1024)S(1)}, f32[1280]{0:T(1024)}, u32[]{:S(2)}) copy-start(f32[1280]{0:T(1024)} %param.31) | copy-start | bytes 15364
  465.5 127.0 %all-gather.16.cloned.1.call-start = ((), (), s32[]{:S(2)}) async-start(), calls=%async_computation.13 | async-start | bytes 4915200 | tf_op jit(solution)/shard_map/all_gather | solution.py:59
  466.1 187.5 %all-gather.18.cloned.1.call-start = ((), (), s32[]{:S(2)}) async-start(), calls=%async_computation.15 | async-start | bytes 5120000 | tf_op jit(solution)/shard_map/all_gather | solution.py:68
  467.2 350.3 %reduce-scatter.13.cloned.1.call-start = ((), (), s32[]{:S(2)}) async-start(), calls=%async_computation.16 | async-start | bytes 10240000 | tf_op jit(solution)/shard_map/reduce_scatter | solution.py:91
  653.6 16.2 %copy-start.46 = (bf16[1280,1280]{1,0:T(8,128)(2,1)S(1)}, bf16[1280,1280]{1,0:T(8,128)(2,1)}, u32[]{:S(2)}) copy-start(bf16[1280,1280]{1,0:T(8,128)(2,1)} %all-gather.14.cloned.1.call-done) | copy-start | bytes 9830404
  677.5 284.5 %reduce-scatter.11.cloned.1.call-start = ((), (), s32[]{:S(2)}) async-start(), calls=%async_computation.14 | async-start | bytes 10240000 | tf_op jit(solution)/shard_map/reduce_scatter | solution.py:78
  687.8 274.1 %copy-start.32 = (f32[2,196]{1,0:T(2,128)S(1)}, f32[2,196]{1,0:T(2,128)}, u32[]{:S(2)}) copy-start(f32[2,196]{1,0:T(2,128)} %copy-done.31) | copy-start | bytes 4708
  687.8 274.1 %copy-start.44 = (f32[1280]{0:T(1024)S(1)}, f32[1280]{0:T(1024)}, u32[]{:S(2)}) copy-start(f32[1280]{0:T(1024)} %param.33) | copy-start | bytes 15364
  687.9 362.6 %all-gather.20.cloned.1.call-start = ((), (), s32[]{:S(2)}) async-start(), calls=%async_computation.17 | async-start | bytes 5120000 | tf_op jit(solution)/shard_map/all_gather | solution.py:68
  962.0 5.2 copy-start.17
  970.5 229.5 %reduce-scatter.21.cloned.1.call-start = ((), (), s32[]{:S(2)}) async-start(), calls=%async_computation.21 | async-start | bytes 9830400 | tf_op jit(solution)/shard_map/reduce_scatter | solution.py:269
  981.5 218.6 %reduce-scatter.23.cloned.1.call-start = ((), (), s32[]{:S(2)}) async-start(), calls=%async_computation.22 | async-start | bytes 9830400 | tf_op jit(solution)/shard_map/reduce_scatter | solution.py:270
  992.5 57.9 %copy-start.22 = (bf16[320,1280]{1,0:T(8,128)(2,1)S(1)}, bf16[320,1280]{1,0:T(8,128)(2,1)}, u32[]{:S(2)}) copy-start(bf16[320,1280]{1,0:T(8,128)(2,1)} %all_gather.30) | copy-start | bytes 2457604
  992.6 207.5 %reduce-scatter.19.cloned.1.call-start = ((), (), s32[]{:S(2)}) async-start(), calls=%async_computation.20 | async-start | bytes 2457600 | tf_op jit(solution)/shard_map/reduce_scatter | solution.py:268
  1055.7 6.6 copy-start.11
  1062.3 8.5 slice-start
  1065.1 5.7 slice-start.1
  1082.2 33.3 %copy-start.14 = (bf16[8,4,80,196]{3,2,1,0:T(8,128)(2,1)S(1)}, bf16[8,4,80,196]{3,2,1,0:T(8,128)(2,1)}, u32[]{:S(2)}) copy-start(bf16[8,4,80,196]{3,2,1,0:T(8,128)(2,1)} %copy-done.13) | copy-start | bytes 3010564
  1120.6 20.5 %copy-start.3 = (bf16[8,196,1,320]{1,3,0,2:T(8,128)(2,1)S(1)}, bf16[8,196,1,320]{1,3,0,2:T(8,128)(2,1)}, u32[]{:S(2)}) copy-start(bf16[8,196,1,320]{1,3,0,2:T(8,128)(2,1)} %copy-done.2) | copy-start | bytes 3010564
  1140.8 59.3 %reduce-scatter.17.cloned.1.call-start = ((), (), s32[]{:S(2)}) async-start(), calls=%async_computation.19 | async-start | bytes 7372800 | tf_op jit(solution)/shard_map/reduce_scatter | solution.py:267
  1164.5 7.4 copy-start.34
  1168.2 5.9 copy-start.4
  1168.2 5.9 copy-start.12
  1188.6 156.2 %reduce-scatter.15.cloned.1.call-start = ((), (), s32[]{:S(2)}) async-start(), calls=%async_computation.18 | async-start | bytes 10240000 | tf_op jit(solution)/shard_map/reduce_scatter | solution.py:91
  1200.0 347.9 %all-reduce.5.cloned.1.call-start = ((), (), s32[]{:S(2)}) async-start(), calls=%async_computation.23 | async-start | bytes 19660800 | tf_op jit(solution)/shard_map/psum | solution.py:272
  1206.8 138.0 %copy-start.6 = (bf16[2,196,1280]{2,0,1:T(2,128)(2,1)S(1)}, bf16[2,196,1280]{2,0,1:T(2,128)(2,1)}, u32[]{:S(2)}) copy-start(bf16[2,196,1280]{2,0,1:T(2,128)(2,1)} %param.17) | copy-start | bytes 3010564
  1206.8 138.0 %copy-start.27 = (f32[1280]{0:T(1024)S(1)}, f32[1280]{0:T(1024)}, u32[]{:S(2)}) copy-start(f32[1280]{0:T(1024)} %param.20) | copy-start | bytes 15364
  1206.8 138.0 %copy-start.29 = (f32[2,196]{1,0:T(2,128)S(1)}, f32[2,196]{1,0:T(2,128)}, u32[]{:S(2)}) copy-start(f32[2,196]{1,0:T(2,128)} %copy-done.28) | copy-start | bytes 4708
  1233.1 114.0 %copy-start.40 = (f32[2,196]{1,0:T(2,128)S(1)}, f32[2,196]{1,0:T(2,128)}, u32[]{:S(2)}) copy-start(f32[2,196]{1,0:T(2,128)} %copy-done.39) | copy-start | bytes 4708
  1233.1 114.0 %copy-start.36 = (f32[1280]{0:T(1024)S(1)}, f32[1280]{0:T(1024)}, u32[]{:S(2)}) copy-start(f32[1280]{0:T(1024)} %param.27) | copy-start | bytes 15364
  1233.1 114.0 %copy-start.38 = (f32[2,196]{1,0:T(2,128)S(1)}, f32[2,196]{1,0:T(2,128)}, u32[]{:S(2)}) copy-start(f32[2,196]{1,0:T(2,128)} %copy-done.37) | copy-start | bytes 4708
  (18 other events, 53.5 us)
Sparse Core Ops, SparseCore 0:
  9.6 13.7 all-gather.9
  25.5 80.2 all-gather.7
  321.8 139.9 reduce-scatter.8
  463.3 12.9 all-gather.13
  478.4 80.2 all-gather.11
  560.2 10.7 all-gather.15
  573.2 80.2 all-gather.17
  677.6 139.9 reduce-scatter.12
  819.9 142.0 reduce-scatter.10
  970.6 79.7 all-gather.19
  1052.9 13.3 reduce-scatter.20
  1068.4 15.9 reduce-scatter.22
  1140.9 7.4 reduce-scatter.18
  1188.7 11.1 reduce-scatter.16
  1202.2 142.5 reduce-scatter.14
  1349.1 198.7 all-reduce.4
where the time goes:
time: 1580 us; the launch traced here: 1560 us
  waiting for transfers between devices  970 us (61%)
  local copies, waits for them, and re-layouts  245 us (16%)
  matrix products  189 us (12%)
  other arithmetic  72.6 us (5%)
  blocking collectives  70.7 us (4%)
    reduce_scatter x2, waiting for transfers between devices, sum_branch(): lax.psum_scatter(term(jnp.int32(0), own_windows * lax.axis_size('col')),...  284 us
    reduce_scatter x2, waiting for transfers between devices, sum_input(): lax.psum_scatter(term(jnp.int32(0), own_windows * lax.axis_size('col')),...  239 us
    all_gather x2, waiting for transfers between devices, gather_tokens(): return lax.all_gather(normed, 'col', axis=0, tiled=True)  165 us
    psum x1, waiting for transfers between devices, per_device(): lax.psum((qkv_rows, proj_rows, expand_rows, shrink_rows), 'dp')  145 us
    add x6, local copies, waits for them, and re-layouts, attention_scores(): score_sum + rel_rows[:, :, :, :, :, None] + rel_cols[:, :, :, :, None, :]  127 us
    all_gather x2, waiting for transfers between devices, gather_grads(): return lax.all_gather(grad_low, 'col', axis=0, tiled=True)  118 us
    psum x1, blocking collectives, per_device(): lax.psum((first_gain_grad, first_shift_grad, second_gain_grad, second_shi...  43.4 us
    reshape x2, local copies, waits for them, and re-layouts, relative_back(): score_float.reshape(window_count, head_count, span_size, span_size, span_...  41.4 us
  transfers between devices with their start and end apart: 16, of which 11 were waited for; matrix products, arithmetic and copies ran while one was open for 16% of the time, Pallas kernels for 0%

commit v1 on v0

--- a/solution.py
+++ b/solution.py
@@ -1,7 +1,925 @@
+import functools
+
 import jax
 import jax.numpy as jnp
 from jax import lax
+from jax.experimental import pallas as pl
+from jax.experimental.pallas import tpu as pltpu
 from jax.sharding import PartitionSpec as P
+
+BF = jnp.bfloat16
+F32 = jnp.float32
+LANES = 128
+SIDE = 14
+SIDE_PAD = 16
+WROWS = SIDE * SIDE_PAD
+HEAD = 80
+AT_H = HEAD
+AT_W = HEAD + SIDE
+AT_MASK = HEAD + 2 * SIDE
+COL_W = 64
+
+
+def dot(a, b):
+    return jnp.dot(a, b, preferred_element_type=F32)
+
+
+def dot_nt(a, b):
+    return lax.dot_general(a, b, (((1,), (1,)), ((), ())), preferred_element_type=F32)
+
+
+def dot_tn(a, b):
+    return lax.dot_general(a, b, (((0,), (0,)), ((), ())), preferred_element_type=F32)
+
+
+def lane_ids():
+    return lax.broadcasted_iota(jnp.int32, (WROWS, LANES), 1)
+
+
+def row_ids():
+    return lax.broadcasted_iota(jnp.int32, (WROWS, LANES), 0)
+
+
+def key_codes():
+    u = jnp.arange(WROWS)[:, None]
+    lane = jnp.arange(LANES)[None, :]
+    k, l = u // SIDE_PAD, u % SIDE_PAD
+    height = lane - AT_H == k
+    width = (lane - AT_W == l) & (l < SIDE)
+    width_back = (AT_W + SIDE - 1 - lane == l) & (l < SIDE)
+    plain = jnp.where(height | width, 1.0, 0.0)
+    masked = jnp.where((lane == AT_MASK) & (l >= SIDE), -1e30, plain)
+    back = jnp.where(height | width_back, 1.0, 0.0)
+    return jnp.stack([masked, plain, back]).astype(BF)
+
+
+def split_low(values):
+    high = values.astype(BF)
+    return high, (values - high.astype(F32)).astype(BF)
+
+
+def relative_tables(rel_height, rel_width):
+    count = rel_height.shape[0]
+    forward = jnp.zeros((LANES, LANES), F32)
+    forward = forward.at[:HEAD, :count].set(rel_height[::-1].T)
+    forward = forward.at[:HEAD, COL_W : COL_W + count].set(rel_width[::-1].T)
+    high, rest = split_low(forward * (HEAD**0.5))
+    back = jnp.zeros((LANES, LANES), F32)
+    back = back.at[:count, :HEAD].set(rel_height[::-1])
+    back = back.at[COL_W : COL_W + count, :HEAD].set(rel_width)
+    back_high, back_rest = split_low(back)
+    return jnp.concatenate([high, rest]), jnp.concatenate([back_high, back_high, back_rest])
+
+
+def query_codes(query, rel_query):
+    full = dot(jnp.concatenate([query, query], axis=1), rel_query)
+    tiles = full.reshape(SIDE, SIDE_PAD, LANES)
+    heights = jnp.concatenate(
+        [pltpu.roll(tiles[i], AT_H - (SIDE - 1 - i), 1) for i in range(SIDE)], axis=0
+    )
+    widths = pltpu.roll(
+        tiles, AT_W - COL_W - (SIDE - 1), 2, stride=1, stride_axis=1
+    ).reshape(WROWS, LANES)
+    lane = lane_ids()
+    codes = jnp.where(
+        (lane >= AT_H) & (lane < AT_W),
+        heights,
+        jnp.where((lane >= AT_W) & (lane < AT_MASK), widths, 0.0),
+    )
+    high, rest = split_low(codes)
+    first = query + high + jnp.where(lane == AT_MASK, 1.0, 0.0).astype(BF)
+    return jnp.concatenate([first, rest], axis=1)
+
+
+def softmax_rows(query, key, rel_query, codes_ref):
+    left = query_codes(query, rel_query)
+    right = jnp.concatenate([key + codes_ref[0], codes_ref[1]], axis=1)
+    scores = dot_nt(left, right)
+    top = jnp.max(scores, axis=1, keepdims=True)
+    weights = jnp.exp((scores - top) * (HEAD**-0.5))
+    return weights / jnp.sum(weights, axis=1, keepdims=True)
+
+
+def attend(query, key, value, rel_query, codes_ref):
+    probs = softmax_rows(query, key, rel_query, codes_ref)
+    return dot(probs.astype(BF), value)
+
+
+def attend_back(query, key, value, grad, rel_query, rel_back, codes_ref):
+    probs = softmax_rows(query, key, rel_query, codes_ref)
+    prob_grad = dot_nt(grad, value)
+    inner = jnp.sum(probs * prob_grad, axis=1, keepdims=True)
+    score_low = (probs * (prob_grad - inner)).astype(BF)
+    value_grad = dot_tn(probs.astype(BF), grad)
+    key_grad = dot_tn(score_low, query) * (HEAD**-0.5)
+    mixed = dot(score_low, key + codes_ref[2])
+    tiles = mixed.reshape(SIDE, SIDE_PAD, LANES)
+    heights = jnp.concatenate(
+        [pltpu.roll(tiles[i], (SIDE - 1 - i - AT_H) % LANES, 1) for i in range(SIDE)], axis=0
+    )
+    widths = pltpu.roll(
+        tiles, (COL_W - AT_W) % LANES, 2, stride=1, stride_axis=1
+    ).reshape(WROWS, LANES)
+    lane, row = lane_ids(), row_ids()
+    first_h = SIDE - 1 - row // SIDE_PAD
+    first_w = COL_W + row % SIDE_PAD
+    offsets = jnp.where(
+        (lane >= first_h) & (lane < first_h + SIDE),
+        heights,
+        jnp.where((lane >= first_w) & (lane < first_w + SIDE), widths, 0.0),
+    )
+    high, rest = split_low(offsets)
+    query_grad = jnp.where(lane < HEAD, mixed, 0.0) * (HEAD**-0.5) + dot(
+        jnp.concatenate([high, rest, high], axis=1), rel_back
+    )
+    rel_grad = dot_tn(jnp.concatenate([high, rest], axis=1), query)
+    return query_grad, key_grad, value_grad, rel_grad
+
+
+def pad_head(piece):
+    return jnp.concatenate([piece, jnp.zeros((piece.shape[0], LANES - HEAD), piece.dtype)], axis=1)
+
+
+def qkv_low(s, rows, h1, wq, bias, half):
+    return (dot(h1[rows, :half], block(wq, s, 0)) + dot(h1[rows, half:], block(wq, s, 1)) + bias).astype(BF)
+
+
+def head_of(low, part, heads, hh):
+    at = (part * heads + hh) * HEAD
+    return pad_head(low[:, at : at + HEAD])
+
+
+def attention_slab(s, h1, wq, wp, bias, rel_query, codes, attended, total, heads, half):
+    @pl.loop(0, h1.shape[0] // WROWS)
+    def _(m):
+        rows = pl.ds(pl.multiple_of(m * WROWS, WROWS), WROWS)
+        low = qkv_low(s, rows, h1, wq, bias, half)
+        outs = []
+        for hh in range(heads):
+            query, key, value = (head_of(low, part, heads, hh) for part in range(3))
+            outs.append(attend(query, key, value, rel_query[...], codes)[:, :HEAD])
+        out_low = jnp.concatenate(outs, axis=1).astype(BF)
+        attended[s, rows] = out_low
+        total[rows, :half] += dot(out_low, block(wp, s, 0))
+        total[rows, half:] += dot(out_low, block(wp, s, 1))
+
+
+SQRT_HALF = 0.5**0.5
+PDF_SCALE = 0.3989422804014327
+
+
+def mlp_rows(s, m, h2, gm, we, ws, bias, act, gpre, total, back, bias_grad, half):
+    count = h2.shape[0] // 4
+
+    @pl.loop(0, 2)
+    def _(step):
+        rows = pl.ds(pl.multiple_of((2 * m + step) * count, count), count)
+        pre = dot(h2[rows, :half], block(we, s, 0)) + dot(h2[rows, half:], block(we, s, 1)) + bias
+        cdf = 0.5 + 0.5 * lax.erf(pre * SQRT_HALF)
+        slope = cdf + pre * (PDF_SCALE * jnp.exp(-0.5 * pre * pre))
+        act_low = (pre * cdf).astype(BF)
+        act[rows, :] = act_low
+        hidden = dot_nt(gm[rows, :half], block(ws, s, 0)) + dot_nt(gm[rows, half:], block(ws, s, 1))
+        gpre_low = (hidden * slope).astype(BF)
+        gpre[rows, :] = gpre_low
+        bias_grad[s] += jnp.sum(gpre_low.astype(F32), axis=0, keepdims=True)
+        total[rows, :half] += dot(act_low, block(ws, s, 0))
+        total[rows, half:] += dot(act_low, block(ws, s, 1))
+        back[rows, :half] += dot_nt(gpre_low, block(we, s, 0))
+        back[rows, half:] += dot_nt(gpre_low, block(we, s, 1))
+
+
+def attention_back_slab(
+    s, h1, ga, wq, wp, bias, rel_query, rel_back, codes, gqkv, back, bias_grad, rel_grad, heads, half
+):
+    @pl.loop(0, h1.shape[0] // WROWS)
+    def _(m):
+        rows = pl.ds(pl.multiple_of(m * WROWS, WROWS), WROWS)
+        low = qkv_low(s, rows, h1, wq, bias, half)
+        grad = (dot_nt(ga[rows, :half], block(wp, s, 0)) + dot_nt(ga[rows, half:], block(wp, s, 1))).astype(BF)
+        parts = [[], [], []]
+        for hh in range(heads):
+            query, key, value = (head_of(low, part, heads, hh) for part in range(3))
+            got = attend_back(
+                query, key, value, head_of(grad, 0, heads, hh), rel_query[...], rel_back[...], codes
+            )
+            for part in range(3):
+                parts[part].append(got[part][:, :HEAD])
+            rel_grad[...] += got[3]
+        grad_low = jnp.concatenate(parts[0] + parts[1] + parts[2], axis=1).astype(BF)
+        gqkv[rows, :] = grad_low
+        bias_grad[s] += jnp.sum(grad_low.astype(F32), axis=0, keepdims=True)
+        back[rows, :half] += dot_nt(grad_low, block(wq, s, 0))
+        back[rows, half:] += dot_nt(grad_low, block(wq, s, 1))
+
+
+MESH_ID = pl.DeviceIdType.MESH
+ARRAYS = ("qkv", "proj", "expand", "shrink")
+CHUNK = 64
+EPS = 1e-06
+SMALL_ROWS = 24
+SPARE = 4
+
+
+def halves(rows):
+    first = (rows // 2 + 15) // 16 * 16
+    return first, rows - first
+
+
+def flip(index, k):
+    return ((index // 2 + k // 2) % 2) * 2 + (index % 2 + k % 2) % 2
+
+
+def block(ref, slab, half):
+    value = ref[slab, half]
+    return value.reshape(value.shape[0] * value.shape[1], value.shape[2])
+
+
+def add_low(target, index, extra):
+    target[index] = (target[index].astype(F32) + extra.astype(F32)).astype(BF)
+
+
+def kernel(
+    tokens, keep, out_grad, vectors, biases, codes, rel_query, rel_back,
+    qkv_src, proj_src, expand_src, shrink_src,
+    block_out, input_grad, qkv_out, proj_out, expand_out, shrink_out, small_out, rel_out,
+    rxq, rxp, rxe, rxs, ryq, ryp, rye, rys, rx2q, rx2p, rx2e, rx2s, ry2q, ry2p, ry2e, ry2s, rzq, rzp, rze, rzs,
+    wq, wp, we, ws, h1, gm, h2, attended, total, back, xr, xr2, middle, act, gpre, gqkv, tmp, tmpq,
+    bias_all, small, small_got, rel, rel_got, bias_e, bias_q, rel_acc,
+    gsend, grecv, rsend, rrecv, fsend, frecv, csend, crecv, zsend, zrecv, local,
+):
+    d, r, z = lax.axis_index("dp"), lax.axis_index("row"), lax.axis_index("col")
+    h, b = d // 2, d % 2
+    own = tokens.shape[0]
+    width = tokens.shape[1]
+    half = width // 2
+    heads = 2
+    bufs = (wq, wp, we, ws)
+    outs = (qkv_out, proj_out, expand_out, shrink_out)
+    rx, ry = (rxq, rxp, rxe, rxs), (ryq, ryp, rye, rys)
+    rx2, ry2 = (rx2q, rx2p, rx2e, rx2s), (ry2q, ry2p, ry2e, ry2s)
+    rz = (rzq, rzp, rze, rzs)
+    parts = [halves(buf.shape[3]) for buf in bufs]
+    attn, mlp = (0, 1), (2, 3)
+
+    along_x = (h * 2 + 1 - b, r, z)
+    along_y = ((1 - h) * 2 + b, r, z)
+    partner = (d, 1 - r, z)
+
+    def along_z(k):
+        return (d, r, flip(z, k))
+
+    def remote(src, dst, sems, recvs, index, device):
+        return pltpu.make_async_remote_copy(
+            src_ref=src,
+            dst_ref=dst,
+            send_sem=sems.at[index],
+            recv_sem=recvs.at[index],
+            device_id=device,
+            device_id_type=MESH_ID,
+        )
+
+    def first_part(a):
+        return pl.ds(0, parts[a][0])
+
+    def second_part(a):
+        return pl.ds(parts[a][0], parts[a][1])
+
+    def gather_z(a, k, arriving=False):
+        at = bufs[a].at[flip(z, k) if arriving else z, h, b]
+        return remote(at, at, gsend, grecv, (a, k, 0), along_z(k))
+
+    def ring(a, slab, sends, recvs, index, kind, arriving):
+        buf = bufs[a]
+        if kind == 1:
+            at, device = (buf.at[slab, h, 1 - b] if arriving else buf.at[slab, h, b]), along_x
+        elif kind == 2:
+            at, device = (buf.at[slab, 1 - h, b] if arriving else buf.at[slab, h, b]), along_y
+        elif kind == 3:
+            at = buf.at[slab, 1 - h if arriving else h, 1 - b, first_part(a)]
+            device = along_y
+        else:
+            at = buf.at[slab, 1 - h, 1 - b if arriving else b, second_part(a)]
+            device = along_x
+        return remote(at, at, sends, recvs, index, device)
+
+    def gather(a, k, kind, arriving=False):
+        return ring(a, flip(z, k), gsend, grecv, (a, k, kind), kind, arriving)
+
+    def spread(a, kind, arriving=False):
+        return ring(a, 3 - z, fsend, frecv, (a, kind), kind, arriving)
+
+    def start_z(group, k):
+        for a in group:
+            gather_z(a, k).start()
+
+    def pass_xy(group, k):
+        for a in group:
+            gather_z(a, k, True).wait_recv()
+            gather(a, k, 1).start()
+            gather(a, k, 2).start()
+
+    def pass_diagonal(group, k):
+        for a in group:
+            gather(a, k, 1, True).wait_recv()
+            gather(a, k, 3).start()
+            gather(a, k, 2, True).wait_recv()
+            gather(a, k, 4).start()
+
+    def finish_slab(group, k):
+        for a in group:
+            gather(a, k, 3, True).wait_recv()
+            gather(a, k, 4, True).wait_recv()
+
+    def sent_z(group):
+        for a in group:
+            for k in (1, 2, 3):
+                gather_z(a, k).wait_send()
+
+    def sent_xy(group, k):
+        for a in group:
+            for kind in (1, 2, 3, 4):
+                gather(a, k, kind).wait_send()
+
+    def slot(k):
+        first = (4 - k) // 4
+        return first * SPARE + (1 - first) * flip(z, k - 1 + first)
+
+    def reduce_copy(a, k, kind):
+        buf, g = bufs[a], slot(k)
+        if kind == 0:
+            src, dst, device = buf.at[g, :, 1 - b, first_part(a)], rx[a].at[k], along_x
+        elif kind == 1:
+            src, dst, device = buf.at[g, 1 - h, :, second_part(a)], ry[a].at[k], along_y
+        elif kind == 2:
+            src, dst, device = buf.at[g, 1 - h, b, first_part(a)], ry2[a].at[k], along_y
+        elif kind == 3:
+            src, dst, device = buf.at[g, h, 1 - b, second_part(a)], rx2[a].at[k], along_x
+        else:
+            src, dst, device = buf.at[g, h, b], rz[a].at[k], along_z(k)
+        return remote(src, dst, rsend, rrecv, (a, k, kind), device)
+
+    def reduce_one(group, k):
+        for a in group:
+            reduce_copy(a, k, 0).start()
+            reduce_copy(a, k, 1).start()
+
+    def scratch(a, place):
+        if a == 0:
+            return tmpq.at[place]
+        return tmp.at[place + (2 if a == 3 else 0)]
+
+    def reduce_two(group, k):
+        loads = []
+        for a in group:
+            reduce_copy(a, k, 0).wait_recv()
+            reduce_copy(a, k, 1).wait_recv()
+            for place, got in enumerate((rx[a], ry[a])):
+                to = scratch(a, place).at[:, pl.ds(0, parts[a][place])]
+                loads.append(pltpu.make_async_copy(got.at[k], to, local.at[a * 2 + place]))
+                loads[-1].start()
+        g = slot(k)
+        for i, a in enumerate(group):
+            first, second = parts[a]
+            loads[2 * i].wait()
+            for side in range(2):
+                add_low(bufs[a], (g, side, b, first_part(a)), scratch(a, 0)[side, :first])
+            reduce_copy(a, k, 2).start()
+            loads[2 * i + 1].wait()
+            for side in range(2):
+                add_low(bufs[a], (g, h, side, second_part(a)), scratch(a, 1)[side, :second])
+            reduce_copy(a, k, 3).start()
+
+    def reduce_three(group, k):
+        loads = []
+        for a in group:
+            reduce_copy(a, k, 2).wait_recv()
+            reduce_copy(a, k, 3).wait_recv()
+            for place, got in enumerate((ry2[a], rx2[a])):
+                to = scratch(a, place).at[0, pl.ds(0, parts[a][place])]
+                loads.append(pltpu.make_async_copy(got.at[k], to, local.at[a * 2 + place]))
+                loads[-1].start()
+        g = slot(k)
+        for i, a in enumerate(group):
+            first, second = parts[a]
+            loads[2 * i].wait()
+            add_low(bufs[a], (g, h, b, first_part(a)), scratch(a, 0)[0, :first])
+            loads[2 * i + 1].wait()
+            add_low(bufs[a], (g, h, b, second_part(a)), scratch(a, 1)[0, :second])
+
+            @pl.when(k > 0)
+            def _():
+                reduce_copy(a, k, 4).start()
+
+    def reduce_four(group):
+        for a in group:
+            rows = bufs[a].shape[3]
+            hold = gqkv if a == 0 else act
+            loads = []
+            for k in (1, 2, 3):
+                got = remote(bufs[a].at[slot(k), h, b], rz[a].at[k], rsend, rrecv, (a, k, 4), along_z(k))
+                got.wait_recv()
+                loads.append(
+                    pltpu.make_async_copy(rz[a].at[k], hold.at[pl.ds((k - 1) * rows, rows)], local.at[k])
+                )
+                loads[-1].start()
+            for load in loads:
+                load.wait()
+            value = bufs[a][SPARE, h, b].astype(F32)
+            for k in range(3):
+                value = value + hold[k * rows : (k + 1) * rows].astype(F32)
+            bufs[a][3 - z, h, b] = value.astype(BF)
+            spread(a, 1).start()
+            spread(a, 2).start()
+
+    def reduce_five(group):
+        for a in group:
+            spread(a, 1, True).wait_recv()
+            spread(a, 3).start()
+            spread(a, 2, True).wait_recv()
+            spread(a, 4).start()
+
+    def swap_out(a):
+        return remote(bufs[a].at[3 - z, 1 - r], outs[a].at[r], fsend, frecv, (a, 0), partner)
+
+    def keep_out(a):
+        return pltpu.make_async_copy(bufs[a].at[3 - z, r], outs[a].at[r], local.at[a])
+
+    def reduce_six(group):
+        for a in group:
+            spread(a, 3, True).wait_recv()
+            spread(a, 4, True).wait_recv()
+            swap_out(a).start()
+            keep_out(a).start()
+
+    def exchange(index, src, dst):
+        return remote(src, dst, csend, crecv, index, partner)
+
+    rows_own, rows_other = pl.ds(0, own), pl.ds(own, own)
+    sources = (
+        lambda side: qkv_src.at[side],
+        lambda side: proj_src.at[side],
+        lambda side: expand_src.at[:, :, pl.ds(pl.multiple_of(side * half, half), half)],
+        lambda side: shrink_src.at[side],
+    )
+
+    def source_swap(a):
+        return exchange(a, sources[a](1 - r), bufs[a].at[z, r])
+
+    def source_keep(a):
+        return pltpu.make_async_copy(sources[a](r), bufs[a].at[z, r], local.at[a])
+
+    grad_load = pltpu.make_async_copy(out_grad, gm.at[rows_own], local.at[4])
+    swap_grad = exchange(4, out_grad, gm.at[rows_other])
+    swap_h1 = exchange(5, h1.at[rows_own], h1.at[rows_other])
+    swap_attn = exchange(6, total.at[rows_other], xr)
+    swap_h2 = exchange(7, h2.at[rows_own], h2.at[rows_other])
+    swap_mlp = exchange(8, total.at[rows_other], xr)
+    swap_gh2 = exchange(9, back.at[rows_other], xr2)
+    swap_ga = exchange(10, gm.at[rows_own], gm.at[rows_other])
+    swap_gh1 = exchange(11, back.at[rows_other], xr)
+
+    def bias_copy(k, arriving=False):
+        at = bias_all.at[flip(z, k) if arriving else z]
+        return remote(at, at, zsend, zrecv, k, along_z(k))
+
+    barrier = pltpu.get_barrier_semaphore()
+    peers = [partner, along_x, along_y, along_z(1), along_z(2), along_z(3)]
+    for peer in peers:
+        pl.semaphore_signal(barrier, inc=1, device_id=peer, device_id_type=MESH_ID)
+    pl.semaphore_wait(barrier, len(peers))
+
+    for a in range(4):
+        source_swap(a).start()
+        source_keep(a).start()
+    bias_load = pltpu.make_async_copy(biases, bias_all.at[z], local.at[5])
+    bias_load.start()
+    grad_load.start()
+    swap_grad.start()
+    bias_load.wait()
+    for k in (1, 2, 3):
+        bias_copy(k).start()
+    for a in attn:
+        source_swap(a).wait()
+        source_keep(a).wait()
+    for k in (1, 2, 3):
+        start_z(attn, k)
+
+    gain_one, shift_one = vectors[0:1, :], vectors[1:2, :]
+    gain_two, shift_two = vectors[2:3, :], vectors[3:4, :]
+    proj_bias, shrink_bias = vectors[4:5, :], vectors[5:6, :]
+
+    def over_rows(body):
+        @pl.loop(0, own // CHUNK)
+        def _(m):
+            body(pl.ds(pl.multiple_of(m * CHUNK, CHUNK), CHUNK))
+
+    def column_sum(value):
+        return jnp.sum(value, axis=0, keepdims=True)
+
+    def normalize(value):
+        center = value - jnp.mean(value, axis=1, keepdims=True)
+        inverse = lax.rsqrt(jnp.mean(center * center, axis=1, keepdims=True) + EPS)
+        return center * inverse, inverse
+
+    def norm_back(grad, gain, xhat, inverse):
+        scaled = grad * gain
+        mean = jnp.mean(scaled, axis=1, keepdims=True)
+        along = jnp.mean(scaled * xhat, axis=1, keepdims=True)
+        return (scaled - mean - xhat * along) * inverse
+
+    small[...] = jnp.zeros_like(small)
+
+    def first_rows(rows):
+        value = tokens[rows].astype(F32)
+        valid = keep[rows]
+        xhat, _ = normalize(value)
+        h1[rows] = ((xhat * gain_one + shift_one) * valid).astype(BF)
+        small[0:1, :] += column_sum(valid * value * value)
+        small[5:6, :] += jnp.broadcast_to(column_sum(valid), (1, width))
+
+    over_rows(first_rows)
+    swap_h1.start()
+    total[...] = jnp.zeros_like(total)
+    for k in (1, 2, 3):
+        bias_copy(k, True).wait_recv()
+    swap_h1.wait_recv()
+
+    def bias_q_of(s):
+        return bias_all[s, 0:1, half : half + wq.shape[4]]
+
+    def bias_e_of(s):
+        return bias_all[s, 0:1, :half]
+
+    @pl.loop(0, 4)
+    def _(k):
+        s = flip(z, k)
+
+        @pl.when(k > 0)
+        def _():
+            pass_diagonal(attn, k)
+            finish_slab(attn, k)
+
+        attention_slab(
+            s, h1, wq, wp, bias_q_of(s), rel_query, codes, attended, total, heads, half
+        )
+
+        @pl.when(k == 0)
+        def _():
+            pass_xy(attn, 1)
+            for a in mlp:
+                source_swap(a).wait()
+                source_keep(a).wait()
+            start_z(mlp, 1)
+
+        @pl.when(k < 2)
+        def _():
+            pass_xy(attn, k + 2)
+            start_z(mlp, k + 2)
+
+        @pl.when(k >= 2)
+        def _():
+            pass_xy(mlp, k - 1)
+
+    swap_attn.start()
+    swap_attn.wait()
+
+    def middle_rows(rows):
+        value = tokens[rows].astype(F32)
+        valid = keep[rows]
+        attn_out = total[rows] + xr[rows] + proj_bias
+        mid = value + attn_out
+        middle[rows] = mid
+        xhat, _ = normalize(mid)
+        h2[rows] = (xhat * gain_two + shift_two).astype(BF)
+        small[1:2, :] += column_sum(valid * mid * mid)
+        small[3:4, :] += column_sum(valid * attn_out * attn_out)
+
+    over_rows(middle_rows)
+    swap_h2.start()
+    total[...] = jnp.zeros_like(total)
+    back[...] = jnp.zeros_like(back)
+    bias_e[...] = jnp.zeros_like(bias_e)
+    bias_q[...] = jnp.zeros_like(bias_q)
+    rel_acc[...] = jnp.zeros_like(rel_acc)
+    grad_load.wait()
+    swap_grad.wait()
+    swap_h2.wait()
+
+    @pl.loop(0, 4)
+    def _(k):
+        s = flip(z, k)
+        g = slot(k)
+
+        @pl.when(k > 0)
+        def _():
+            finish_slab(mlp, k)
+
+        mlp_rows(s, 0, h2, gm, we, ws, bias_e_of(s), act, gpre, total, back, bias_e, half)
+
+        @pl.when(k < 3)
+        def _():
+            pass_diagonal(mlp, k + 1)
+
+        mlp_rows(s, 1, h2, gm, we, ws, bias_e_of(s), act, gpre, total, back, bias_e, half)
+
+        @pl.when(k == 1)
+        def _():
+            sent_z(mlp)
+
+        @pl.when(k > 1)
+        def _():
+            sent_xy(mlp, k - 1)
+
+        @pl.when(k == 3)
+        def _():
+            sent_xy(mlp, 3)
+
+        for side in range(2):
+            columns = slice(side * half, side * half + half)
+            we[g, side] = dot_tn(h2[:, columns], gpre[...]).astype(BF).reshape(we.shape[2:])
+            ws[g, side] = dot_tn(act[: 2 * own], gm[:, columns]).astype(BF).reshape(ws.shape[2:])
+        reduce_one(mlp, k)
+
+        @pl.when(k == 1)
+        def _():
+            pass_xy(mlp, 3)
+
+        @pl.when(k > 0)
+        def _():
+            reduce_two(mlp, k - 1)
+
+    swap_mlp.start()
+    swap_gh2.start()
+    reduce_two(mlp, 3)
+    swap_mlp.wait()
+    swap_gh2.wait()
+
+    def result_rows(rows):
+        valid = keep[rows]
+        mid = middle[rows]
+        mlp_out = total[rows] + xr[rows] + shrink_bias
+        result = mid + mlp_out
+        h2[rows] = result.astype(BF)
+        small[2:3, :] += column_sum(valid * result * result)
+        small[4:5, :] += column_sum(valid * mlp_out * mlp_out)
+        grad_out = gm[rows].astype(F32)
+        small[11:12, :] += column_sum(grad_out)
+        grad = back[rows] + xr2[rows]
+        xhat, inverse = normalize(mid)
+        small[8:9, :] += column_sum(grad * xhat)
+        small[9:10, :] += column_sum(grad)
+        grad_mid = grad_out + norm_back(grad, gain_two, xhat, inverse)
+        middle[rows] = grad_mid
+        low = grad_mid.astype(BF)
+        gm[rows] = low
+        small[10:11, :] += column_sum(low.astype(F32))
+
+    over_rows(result_rows)
+    swap_ga.start()
+    result_store = pltpu.make_async_copy(h2.at[rows_own], block_out, local.at[8])
+    result_store.start()
+    back[...] = jnp.zeros_like(back)
+    swap_ga.wait()
+
+    @pl.loop(0, 4)
+    def _(k):
+        s = flip(z, k)
+        g = slot(k)
+        attention_back_slab(
+            s, h1, gm, wq, wp, bias_q_of(s), rel_query, rel_back, codes, gqkv, back, bias_q, rel_acc, heads, half
+        )
+
+        @pl.when(k == 1)
+        def _():
+            sent_z(attn)
+
+        @pl.when(k > 1)
+        def _():
+            sent_xy(attn, k - 1)
+
+        @pl.when(k == 3)
+        def _():
+            sent_xy(attn, 3)
+
+        for side in range(2):
+            columns = slice(side * half, side * half + half)
+            wq[g, side] = dot_tn(h1[:, columns], gqkv[: 2 * own]).astype(BF).reshape(wq.shape[2:])
+            wp[g, side] = dot_tn(attended[s], gm[:, columns]).astype(BF).reshape(wp.shape[2:])
+        reduce_one(attn, k)
+        reduce_three(mlp, k)
+
+        @pl.when(k > 0)
+        def _():
+            reduce_two(attn, k - 1)
+
+    swap_gh1.start()
+    reduce_two(attn, 3)
+    reduce_four(mlp)
+    swap_gh1.wait()
+
+    def input_rows(rows):
+        value = tokens[rows].astype(F32)
+        grad = (back[rows] + xr[rows]) * keep[rows]
+        xhat, inverse = normalize(value)
+        small[6:7, :] += column_sum(grad * xhat)
+        small[7:8, :] += column_sum(grad)
+        middle[rows] = middle[rows] + norm_back(grad, gain_one, xhat, inverse)
+
+    over_rows(input_rows)
+    input_store = pltpu.make_async_copy(middle, input_grad, local.at[9])
+    input_store.start()
+
+    for s in range(4):
+        at = SMALL_ROWS - 8 + s
+        for side in range(2):
+
+            @pl.when(r == side)
+            def _():
+                small[at + 4 * side : at + 4 * side + 1, :half] = bias_e[s]
+                small[at + 4 * side : at + 4 * side + 1, half : half + bias_q.shape[2]] = bias_q[s]
+
+    rel[...] = rel_acc[:LANES] + rel_acc[LANES:]
+
+    def small_step(step, device):
+        first = remote(small, small_got.at[step], csend, crecv, 12 + 2 * step, device)
+        second = remote(rel, rel_got.at[step], csend, crecv, 13 + 2 * step, device)
+        first.start()
+        second.start()
+
+        def finish():
+            first.wait()
+            second.wait()
+            small[...] += small_got[step]
+            rel[...] += rel_got[step]
+
+        return finish
+
+    finish = small_step(0, partner)
+    reduce_three(attn, 0)
+    finish()
+    finish = small_step(1, along_x)
+    reduce_three(attn, 1)
+    reduce_three(attn, 2)
+    finish()
+    finish = small_step(2, along_y)
+    reduce_three(attn, 3)
+    reduce_five(mlp)
+    finish()
+    finish = small_step(3, along_z(1))
+    reduce_four(attn)
+    finish()
+    finish = small_step(4, along_z(2))
+    reduce_six(mlp)
+    reduce_five(attn)
+    finish()
+    small_store = pltpu.make_async_copy(small, small_out, local.at[6])
+    rel_store = pltpu.make_async_copy(rel, rel_out, local.at[7])
+    small_store.start()
+    rel_store.start()
+    reduce_six(attn)
+
+    swap_h1.wait_send()
+    for k in (1, 2, 3):
+        bias_copy(k).wait_send()
+    for a in range(4):
+        swap_out(a).wait()
+        keep_out(a).wait()
+        for kind in (1, 2, 3, 4):
+            spread(a, kind).wait_send()
+        for k in range(4):
+            for kind in range(4):
+                reduce_copy(a, k, kind).wait_send()
+            if k > 0:
+                reduce_copy(a, k, 4).wait_send()
+    small_store.wait()
+    rel_store.wait()
+    result_store.wait()
+    input_store.wait()
+
+
+def run_kernel(
+    tokens, keep, out_grad, vectors, biases, codes, rel_query, rel_back, qkv_src, proj_src, expand_src, shrink_src
+):
+    own, width = tokens.shape
+    sources = (qkv_src, proj_src, expand_src, shrink_src)
+    rows = [qkv_src.shape[2], proj_src.shape[2], expand_src.shape[1], shrink_src.shape[2]]
+    lanes = [qkv_src.shape[3], proj_src.shape[3], width // 2, shrink_src.shape[3]]
+    sds = jax.ShapeDtypeStruct
+    any_spec = pl.BlockSpec(memory_space=pl.ANY)
+    vmem_spec = pl.BlockSpec(memory_space=pltpu.VMEM)
+    out_shape = [sds((own, width), BF), sds((own, width), F32)]
+    out_shape += [sds((2, 2, n, l), BF) for n, l in zip(rows, lanes)]
+    out_shape += [sds((SMALL_ROWS, width), F32), sds((LANES, LANES), F32)]
+    first, second = zip(*[halves(n) for n in rows])
+    out_shape += [sds((4, 2, n, l), BF) for n, l in zip(first, lanes)]
+    out_shape += [sds((4, 2, n, l), BF) for n, l in zip(second, lanes)]
+    out_shape += [sds((4, n, l), BF) for n, l in zip(second, lanes)]
+    out_shape += [sds((4, n, l), BF) for n, l in zip(first, lanes)]
+    out_shape += [sds((4, n, l), BF) for n, l in zip(rows, lanes)]
+    both = 2 * own
+    vmem, dma = pltpu.VMEM, pltpu.SemaphoreType.DMA
+    hidden, qkv_width = lanes[3], lanes[0]
+    scratch = [vmem((5, 2, 2, n, l), BF) for n, l in zip(rows, lanes)]
+    scratch += [vmem((both, width), BF)] * 3
+    scratch += [vmem((4, both, qkv_width // 3), BF)]
+    scratch += [vmem((both, width), F32)] * 2
+    scratch += [vmem((own, width), F32)] * 3
+    deep = max(both, 3 * rows[2])
+    scratch += [vmem((deep, hidden), BF), vmem((both, hidden), BF), vmem((deep, qkv_width), BF)]
+    scratch += [vmem((4, 2, first[2], hidden), BF), vmem((2, 2, first[0], qkv_width), BF)]
+    scratch += [vmem((4, 8, width), F32), vmem((SMALL_ROWS, width), F32), vmem((5, SMALL_ROWS, width), F32)]
+    scratch += [vmem((LANES, LANES), F32), vmem((5, LANES, LANES), F32)]
+    scratch += [vmem((4, 1, hidden), F32), vmem((4, 1, qkv_width), F32), vmem((2 * LANES, LANES), F32)]
+    scratch += [dma((4, 4, 5))] * 4 + [dma((4, 5))] * 2 + [dma((22,))] * 2 + [dma((4,))] * 2 + [dma((10,))]
+    got = pl.pallas_call(
+        kernel,
+        out_shape=out_shape,
+        in_specs=[vmem_spec, vmem_spec, any_spec, vmem_spec, any_spec] + [vmem_spec] * 3 + [any_spec] * 4,
+        out_specs=[any_spec] * len(out_shape),
+        scratch_shapes=scratch,
+        compiler_params=pltpu.CompilerParams(
+            collective_id=0, has_side_effects=True, vmem_limit_bytes=VMEM_LIMIT
+        ),
+        name="block_step",
+    )(tokens, keep, out_grad, vectors, biases, codes, rel_query, rel_back, *sources)
+    return got[:8]
+
+
+VMEM_LIMIT = 64 * 1024 * 1024 - 512 * 1024
+
+
+def over_chips(
+    tokens, valid_mask, out_grad, first_gain, first_shift, qkv_weight, qkv_bias, rel_height, rel_width,
+    proj_weight, proj_bias, second_gain, second_shift, expand_weight, expand_bias, shrink_weight, shrink_bias,
+):
+    windows, per, width = tokens.shape
+    side = (rel_height.shape[0] + 1) // 2
+    count, head = rel_height.shape
+    r = lax.axis_index("row")
+
+    def padded(value):
+        grid = value.reshape(windows, side, side, -1)
+        grid = jnp.pad(grid, ((0, 0), (0, 0), (0, SIDE_PAD - side), (0, 0)))
+        return grid.reshape(windows * side * SIDE_PAD, -1)
+
+    def cut(value):
+        grid = value.reshape(windows, side, SIDE_PAD, -1)[:, :, :side]
+        return grid.reshape(windows, per, -1)
+
+    rows, _, local_width = qkv_weight.shape
+    part = local_width // 2
+    hidden = expand_weight.shape[1] // 2
+    qkv_src = qkv_weight.reshape(rows, 3, 2, part).transpose(2, 0, 1, 3).reshape(2, 2, rows // 2, 3 * part)
+    proj_src = proj_weight.reshape(2, 2, part // 2, proj_weight.shape[1])
+    expand_src = expand_weight.reshape(2, rows // 2, 2 * hidden)
+    shrink_src = shrink_weight.reshape(2, 2, hidden // 2, shrink_weight.shape[1])
+    zeros = jnp.zeros((part,), F32)
+    query_bias, value_bias = (lax.dynamic_slice_in_dim(qkv_bias[i], r * part, part) for i in range(2))
+    bias = jnp.concatenate(
+        [lax.dynamic_slice_in_dim(expand_bias, r * hidden, hidden), query_bias, zeros, value_bias]
+    )
+    biases = jnp.pad(bias[None], ((0, 7), (0, width - bias.shape[0])))
+    vectors = jnp.stack([first_gain, first_shift, second_gain, second_shift, proj_bias, shrink_bias])
+    vectors = jnp.pad(vectors, ((0, 2), (0, 0)))
+    rel_query, rel_back = relative_tables(rel_height, rel_width)
+    keep = padded(valid_mask.astype(F32))
+    got = run_kernel(
+        padded(tokens), keep, padded(out_grad), vectors, biases, key_codes(), rel_query, rel_back,
+        qkv_src, proj_src, expand_src, shrink_src,
+    )
+    block_low, grad, qkv_got, proj_got, expand_got, shrink_got, small, rel = got
+    qkv_sum = qkv_got.astype(F32).reshape(2, rows, 3, part).transpose(1, 2, 0, 3).reshape(rows, 3, 2 * part)
+    proj_sum = proj_got.astype(F32).reshape(2 * part, -1)
+    expand_sum = expand_got.astype(F32).reshape(2, rows, hidden).transpose(1, 0, 2).reshape(rows, 2 * hidden)
+    shrink_sum = shrink_got.astype(F32).reshape(2 * hidden, -1)
+    rms = jnp.sqrt(jnp.sum(small[:5], axis=1) / (small[5, 0] * width))
+    slabs = small[SMALL_ROWS - 8 :].reshape(2, 4, width)
+    mine = lax.dynamic_index_in_dim(slabs, lax.axis_index("col"), axis=1, keepdims=False)
+    expand_bias_sum = mine[:, :hidden].reshape(-1)
+    qkv_bias_sum = mine[:, hidden : hidden + 3 * part].reshape(2, 3, part)[:, 0::2].transpose(1, 0, 2).reshape(2, -1)
+    height_sum = rel[:count, :head][::-1]
+    width_sum = rel[COL_W : COL_W + count, :head]
+    return (
+        cut(block_low),
+        cut(grad),
+        small[6],
+        small[7],
+        qkv_sum,
+        qkv_bias_sum,
+        height_sum,
+        width_sum,
+        proj_sum,
+        small[10],
+        small[8],
+        small[9],
+        expand_sum,
+        expand_bias_sum,
+        shrink_sum,
+        small[11],
+        rms,
+    )
+
 
 epsilon = 1e-06
 highest = lax.Precision.HIGHEST
@@ -317,6 +1235,11 @@
     )
 
 
+def choose(mesh):
+    fits = tuple(mesh.shape[name] for name in ("dp", "row", "col")) == (4, 2, 4)
+    return over_chips if fits else per_device
+
+
 def solution(mesh):
     in_specs = (
         P(("dp", "row", "col"), None, None),
@@ -357,5 +1280,5 @@
         P(),
     )
     return jax.shard_map(
-        per_device, mesh=mesh, in_specs=in_specs, out_specs=out_specs, check_vma=False
-    )
+        choose(mesh), mesh=mesh, in_specs=in_specs, out_specs=out_specs, check_vma=False
+    )

time: 1580 us -> 509 us (0.32)
  waiting for transfers between devices: 970 us -> 0 us
  Pallas kernels: 0 us -> 447 us
  local copies, waits for them, and re-layouts: 245 us -> 47.6 us
  matrix products: 189 us -> 0 us
  blocking collectives: 70.7 us -> 0 us
  other arithmetic: 72.6 us -> 9.72 us
    reduce_scatter x8 -> x0, waiting for transfers between devices: 523 us -> none  [the longest x2 284 us: sum_branch(): lax.psum_scatter(term(jnp.int32(0), own_windows * lax.axis_size('col')),...]
    pallas_call x0 -> x1, Pallas kernels: none -> 447 us  [run_kernel(): pl.pallas_call(kernel, out_shape=out_shape, in_specs=[vmem_spec, vmem_spe...]
    all_gather x7 -> x0, waiting for transfers between devices: 299 us -> none  [the longest x2 165 us: gather_tokens(): return lax.all_gather(normed, 'col', axis=0, tiled=True)]
    dot_general x28 -> x0, matrix products: 189 us -> none  [the longest x2 18.7 us: term(): jnp.einsum('btk,dk->btd', grads_low, weight_full, preferred_element_type=...]
    psum x1 -> x0, waiting for transfers between devices: 145 us -> none  [per_device(): lax.psum((qkv_rows, proj_rows, expand_rows, shrink_rows), 'dp')]
    add x6 -> x0, local copies, waits for them, and re-layouts: 127 us -> none  [attention_scores(): score_sum + rel_rows[:, :, :, :, :, None] + rel_cols[:, :, :, :, None, :]]
    psum x2 -> x0, blocking collectives: 68.1 us -> none  [the longest x1 43.4 us: per_device(): lax.psum((first_gain_grad, first_shift_grad, second_gain_grad, second_shi...]
    reduce_sum x13 -> x1, other arithmetic: 41 us -> 0.12 us  [over_chips(): rms = jnp.sqrt(jnp.sum(small[:5], axis=1) / (small[5, 0] * width))]
  transfers between devices with their start and end apart: 16 -> 0, of which waited for: 11 -> 0; matrix products, arithmetic and copies ran while one was open for 16% -> 0% of each run, Pallas kernels for 0% -> 0%
where the time goes in v1:
time: 509 us; the launch traced here: 506 us
  Pallas kernels  447 us (88%)
  local copies, waits for them, and re-layouts  47.6 us (9%)
  other arithmetic  9.72 us (2%)
    pallas_call x1, Pallas kernels, run_kernel(): pl.pallas_call(kernel, out_shape=out_shape, in_specs=[vmem_spec, vmem_spe...  447 us
    reshape x3, local copies, waits for them, and re-layouts, over_chips(): qkv_got.astype(F32).reshape(2, rows, 3, part).transpose(1, 2, 0, 3)  10.4 us

profile of v1, /device:TPU:0, one launch (start us, length us, event | category | flops | bytes accessed | tf_op | source)
XLA Modules:
  0.0 505.7 jit_solution(9405279434356613153)
XLA Ops:
  0.7 1.4 and_reduce_fusion
  2.1 0.6 fusion.5
  2.7 0.7 convert_element_type.35
  3.4 0.8 fusion.4
  4.2 0.8 dynamic_slice.17
  5.1 0.7 stack.28
  5.8 0.7 stack.29
  6.5 0.7 stack.32
  7.2 0.7 stack.30
  7.9 0.7 stack.31
  8.6 0.7 stack.33
  9.3 0.6 pad.41.vectors
  10.0 0.7 rev.10
  10.8 0.7 rev.11
  11.5 2.0 fusion.1
  13.5 0.6 pad.42.biases
  14.1 1.9 scatter.15
  16.1 0.7 copy.56.rel_query
  16.9 1.7 scatter.19
  18.6 0.6 pad_maximum_fusion.1.rel_back
  19.2 0.2 fusion
  19.4 0.7 pad_maximum_fusion.codes
  20.1 0.8 reshape.741.keep
  21.1 1.1 pad.38
  22.2 0.5 copy-done.4
  22.7 0.1 copy.53
  22.8 1.1 pad.40
  23.9 0.6 copy-done.2
  24.7 1.2 reshape.705
  25.9 3.4 copy.57.qkv_src
  29.3 446.9 %block_step.1 = (bf16[448,1280]{1,0:T(8,128)(2,1)}, f32[448,1280]{1,0:T(8,128)}, bf16[2,2,320,480]{3,2,1,0:T(8,128)(2,1)}, bf16[2,2,80,640]{3,2,1,0:T(8,128)(2,1...) custom-call(bf16[448,1280]{1,0:T(8,128)(2,1)} %bitcast.54, ...), custom_call_target="tpu_custom_call" | custom-call | tf_op jit(solution)/shard_map/block_step/pallas_call | solution.py:835
  476.2 1.2 slice.162
  478.1 3.2 copy.58
  481.3 4.5 copy.59
  485.9 0.1 slice_reduce_fusion
  486.0 0.5 divide_sqrt_fusion
  486.5 0.6 fusion.3
  487.1 0.6 rev.12
  487.8 0.7 slice_reduce_fusion.1
  488.5 0.6 reshape.724
  489.2 0.7 reshape.718
  489.9 1.0 bitcast_convert_fusion.1
  490.9 4.0 copy.60
  494.9 3.0 reshape.738
  497.9 3.4 copy.61
  501.3 0.4 convert_bitcast_fusion
  501.7 2.0 copy.65
  503.6 2.1 bitcast_convert_fusion
  (43 shorter events, 0.8 us)
Async XLA Ops:
  0.7 20.3 %copy-start.3 = (bf16[2,196,1280]{2,0,1:T(2,128)(2,1)S(1)}, bf16[2,196,1280]{2,0,1:T(2,128)(2,1)}, u32[]{:S(2)}) copy-start(bf16[2,196,1280]{2,0,1:T(2,128)(2,1)} %param.25) | copy-start | bytes 3010564
  21.1 1.6 copy-start.4
  22.8 1.7 copy-start.2
  481.3 4.6 copy-start.6
  481.3 5.2 %copy-start.7 = (f32[128,128]{1,0:T(8,128)S(1)}, f32[128,128]{1,0:T(8,128)}, u32[]{:S(2)}) copy-start(f32[128,128]{1,0:T(8,128)} %get-tuple-element.77) | copy-start | bytes 196612
  481.3 8.6 %copy-start.5 = (bf16[2,2,80,640]{3,2,1,0:T(8,128)(2,1)S(1)}, bf16[2,2,80,640]{3,2,1,0:T(8,128)(2,1)}, u32[]{:S(2)}) copy-start(bf16[2,2,80,640]{3,2,1,0:T(8,128)(2,1)} %get-tuple-element.78) | copy-start | bytes 1228804
  497.9 3.4 copy-start.1
  501.7 2.0 copy-start

commit v2 on v1

--- a/solution.py
+++ b/solution.py
@@ -2,6 +2,7 @@
 
 import jax
 import jax.numpy as jnp
+import numpy as np
 from jax import lax
 from jax.experimental import pallas as pl
 from jax.experimental.pallas import tpu as pltpu
@@ -41,16 +42,16 @@
 
 
 def key_codes():
-    u = jnp.arange(WROWS)[:, None]
-    lane = jnp.arange(LANES)[None, :]
+    u = np.arange(WROWS)[:, None]
+    lane = np.arange(LANES)[None, :]
     k, l = u // SIDE_PAD, u % SIDE_PAD
     height = lane - AT_H == k
     width = (lane - AT_W == l) & (l < SIDE)
     width_back = (AT_W + SIDE - 1 - lane == l) & (l < SIDE)
-    plain = jnp.where(height | width, 1.0, 0.0)
-    masked = jnp.where((lane == AT_MASK) & (l >= SIDE), -1e30, plain)
-    back = jnp.where(height | width_back, 1.0, 0.0)
-    return jnp.stack([masked, plain, back]).astype(BF)
+    plain = np.where(height | width, 1.0, 0.0)
+    masked = np.where((lane == AT_MASK) & (l >= SIDE), -1e30, plain)
+    back = np.where(height | width_back, 1.0, 0.0)
+    return np.stack([masked, plain, back]).astype(BF)
 
 
 def split_low(values):
@@ -58,17 +59,26 @@
     return high, (values - high.astype(F32)).astype(BF)
 
 
-def relative_tables(rel_height, rel_width):
-    count = rel_height.shape[0]
-    forward = jnp.zeros((LANES, LANES), F32)
-    forward = forward.at[:HEAD, :count].set(rel_height[::-1].T)
-    forward = forward.at[:HEAD, COL_W : COL_W + count].set(rel_width[::-1].T)
-    high, rest = split_low(forward * (HEAD**0.5))
-    back = jnp.zeros((LANES, LANES), F32)
-    back = back.at[:count, :HEAD].set(rel_height[::-1])
-    back = back.at[COL_W : COL_W + count, :HEAD].set(rel_width)
-    back_high, back_rest = split_low(back)
-    return jnp.concatenate([high, rest]), jnp.concatenate([back_high, back_high, back_rest])
+def relative_tables(rel_h, rel_w, rel_query, rel_back):
+    count, rows = 2 * SIDE - 1, rel_h.shape[0]
+    offset = lax.broadcasted_iota(jnp.int32, (rows, LANES), 0)
+    lane = lax.broadcasted_iota(jnp.int32, (rows, LANES), 1)
+
+    def places(first, step):
+        return jnp.where((lane == first + step * offset) & (offset < count), 1.0, 0.0).astype(BF)
+
+    heights, widths = places(count - 1, -1), places(COL_W + count - 1, -1)
+    widths_back = places(COL_W, 1)
+    tall, wide = rel_h[...], rel_w[...]
+    rel_query[...] = jnp.zeros_like(rel_query)
+    rel_back[...] = jnp.zeros_like(rel_back)
+    for part, (a, b) in enumerate(zip(split_low(tall * HEAD**0.5), split_low(wide * HEAD**0.5))):
+        at = part * LANES
+        rel_query[at : at + HEAD] = (dot_tn(a, heights) + dot_tn(b, widths)).astype(BF)
+    for part, (a, b) in enumerate(zip(split_low(tall), split_low(wide))):
+        table = (dot_tn(heights, a) + dot_tn(widths_back, b)).astype(BF)
+        for place in ((0, 1), (2,))[part]:
+            rel_back[place * LANES : (place + 1) * LANES, :HEAD] = table
 
 
 def query_codes(query, rel_query):
@@ -141,7 +151,7 @@
 
 
 def qkv_low(s, rows, h1, wq, bias, half):
-    return (dot(h1[rows, :half], block(wq, s, 0)) + dot(h1[rows, half:], block(wq, s, 1)) + bias).astype(BF)
+    return (dot_nt(h1[rows, :half], block(wq, s, 0)) + dot_nt(h1[rows, half:], block(wq, s, 1)) + bias).astype(BF)
 
 
 def head_of(low, part, heads, hh):
@@ -209,8 +219,8 @@
         grad_low = jnp.concatenate(parts[0] + parts[1] + parts[2], axis=1).astype(BF)
         gqkv[rows, :] = grad_low
         bias_grad[s] += jnp.sum(grad_low.astype(F32), axis=0, keepdims=True)
-        back[rows, :half] += dot_nt(grad_low, block(wq, s, 0))
-        back[rows, half:] += dot_nt(grad_low, block(wq, s, 1))
+        back[rows, :half] += dot(grad_low, block(wq, s, 0))
+        back[rows, half:] += dot(grad_low, block(wq, s, 1))
 
 
 MESH_ID = pl.DeviceIdType.MESH
@@ -240,13 +250,13 @@
 
 
 def kernel(
-    tokens, keep, out_grad, vectors, biases, codes, rel_query, rel_back,
-    qkv_src, proj_src, expand_src, shrink_src,
+    tokens, keep, out_grad, gain_one_in, shift_one_in, gain_two_in, shift_two_in, proj_bias_in, shrink_bias_in,
+    qkv_bias_in, expand_bias_in, rel_h_in, rel_w_in, codes, qkv_src, proj_src, expand_src, shrink_src,
     block_out, input_grad, qkv_out, proj_out, expand_out, shrink_out, small_out, rel_out,
     rxq, rxp, rxe, rxs, ryq, ryp, rye, rys, rx2q, rx2p, rx2e, rx2s, ry2q, ry2p, ry2e, ry2s, rzq, rzp, rze, rzs,
-    wq, wp, we, ws, h1, gm, h2, attended, total, back, xr, xr2, middle, act, gpre, gqkv, tmp, tmpq,
-    bias_all, small, small_got, rel, rel_got, bias_e, bias_q, rel_acc,
-    gsend, grecv, rsend, rrecv, fsend, frecv, csend, crecv, zsend, zrecv, local,
+    wq, wp, we, ws, h1, gm, h2, attended, total, back, xr, xr2, middle, act, gpre, gqkv, tmp,
+    bias_all, small, small_got, rel, rel_got, bias_e, bias_q, rel_acc, rel_query, rel_back, rel_pad,
+    gsend, grecv, rsend, rrecv, fsend, frecv, csend, crecv, zsend, zrecv, qsend, qrecv, local, qlocal,
 ):
     d, r, z = lax.axis_index("dp"), lax.axis_index("row"), lax.axis_index("col")
     h, b = d // 2, d % 2
@@ -260,7 +270,7 @@
     rx2, ry2 = (rx2q, rx2p, rx2e, rx2s), (ry2q, ry2p, ry2e, ry2s)
     rz = (rzq, rzp, rze, rzs)
     parts = [halves(buf.shape[3]) for buf in bufs]
-    attn, mlp = (0, 1), (2, 3)
+    attn, mlp, whole, shrink = (0, 1), (2, 3), (2,), (3,)
 
     along_x = (h * 2 + 1 - b, r, z)
     along_y = ((1 - h) * 2 + b, r, z)
@@ -269,25 +279,33 @@
     def along_z(k):
         return (d, r, flip(z, k))
 
-    def remote(src, dst, sems, recvs, index, device):
+    def remote(src, dst, sems, recvs, index, device, got=None):
         return pltpu.make_async_remote_copy(
             src_ref=src,
             dst_ref=dst,
             send_sem=sems.at[index],
-            recv_sem=recvs.at[index],
+            recv_sem=recvs.at[index if got is None else got],
             device_id=device,
             device_id_type=MESH_ID,
         )
 
+    up = z // 2
+    is_end = (z + 1) // 2 % 2 == 0
+    is_inner = (z + 1) // 2 % 2 == 1
+
+    def slab_of(i):
+        far = i // 2
+        return (1 - far) * flip(z, i) + far * ((1 - up) * i + up * (3 - i))
+
     def first_part(a):
         return pl.ds(0, parts[a][0])
 
     def second_part(a):
         return pl.ds(parts[a][0], parts[a][1])
 
-    def gather_z(a, k, arriving=False):
-        at = bufs[a].at[flip(z, k) if arriving else z, h, b]
-        return remote(at, at, gsend, grecv, (a, k, 0), along_z(k))
+    def gather_z(a, s, step):
+        at = bufs[a].at[s] if a in whole else bufs[a].at[s, h, b]
+        return remote(at, at, gsend, grecv, (a, s, 0 if step < 0 else 5), (d, r, z + step), (a, s, 0))
 
     def ring(a, slab, sends, recvs, index, kind, arriving):
         buf = bufs[a]
@@ -303,132 +321,153 @@
             device = along_x
         return remote(at, at, sends, recvs, index, device)
 
-    def gather(a, k, kind, arriving=False):
-        return ring(a, flip(z, k), gsend, grecv, (a, k, kind), kind, arriving)
+    def gather(a, s, kind, arriving=False):
+        return ring(a, s, gsend, grecv, (a, s, kind), kind, arriving)
 
     def spread(a, kind, arriving=False):
-        return ring(a, 3 - z, fsend, frecv, (a, kind), kind, arriving)
-
-    def start_z(group, k):
+        return ring(a, last_slab(a), fsend, frecv, (a, kind), kind, arriving)
+
+    def sends_along_z(group, s, act_on):
         for a in group:
-            gather_z(a, k).start()
-
-    def pass_xy(group, k):
+
+            @pl.when((s >= z) & (z > 0))
+            def _():
+                act_on(gather_z(a, s, -1))
+
+            @pl.when((s <= z) & (z < 3))
+            def _():
+                act_on(gather_z(a, s, 1))
+
+    def start_z(group):
+        sends_along_z(group, z, lambda copy: copy.start())
+
+    def arrive(group, i):
+        s = slab_of(i)
         for a in group:
-            gather_z(a, k, True).wait_recv()
-            gather(a, k, 1).start()
-            gather(a, k, 2).start()
-
-    def pass_diagonal(group, k):
+            gather_z(a, s, 1).wait_recv()
+            sends_along_z((a,), s, lambda copy: copy.start())
+            if a not in whole:
+                gather(a, s, 1).start()
+                gather(a, s, 2).start()
+
+    def pass_diagonal(group, i):
+        s = slab_of(i)
         for a in group:
-            gather(a, k, 1, True).wait_recv()
-            gather(a, k, 3).start()
-            gather(a, k, 2, True).wait_recv()
-            gather(a, k, 4).start()
-
-    def finish_slab(group, k):
+            gather(a, s, 1, True).wait_recv()
+            gather(a, s, 3).start()
+            gather(a, s, 2, True).wait_recv()
+            gather(a, s, 4).start()
+
+    def finish_slab(group, i):
+        s = slab_of(i)
         for a in group:
-            gather(a, k, 3, True).wait_recv()
-            gather(a, k, 4, True).wait_recv()
-
-    def sent_z(group):
+            gather(a, s, 3, True).wait_recv()
+            gather(a, s, 4, True).wait_recv()
+
+    def sent_slab(group, i):
+        s = slab_of(i)
+        sends_along_z(group, s, lambda copy: copy.wait_send())
         for a in group:
-            for k in (1, 2, 3):
-                gather_z(a, k).wait_send()
-
-    def sent_xy(group, k):
+            if a not in whole:
+
+                @pl.when(i > 0)
+                def _():
+                    for kind in (1, 2, 3, 4):
+                        gather(a, s, kind).wait_send()
+
+    def step_slab(a, n):
+        return slab_of(n if a in mlp else 3 - n)
+
+    def last_slab(a):
+        return step_slab(a, 3)
+
+    def slot(a, n):
+        first = (4 - n) // 4
+        return first * SPARE + (1 - first) * step_slab(a, n - 1 + first)
+
+    def reduce_copy(a, n, kind):
+        buf, g = bufs[a], slot(a, n)
+        got = None
+        if kind == 0:
+            src, dst, device = buf.at[g, :, 1 - b, first_part(a)], rx[a].at[n], along_x
+        elif kind == 1:
+            src, dst, device = buf.at[g, 1 - h, :, second_part(a)], ry[a].at[n], along_y
+        elif kind == 2:
+            src, dst, device = buf.at[g, 1 - h, b, first_part(a)], ry2[a].at[n], along_y
+        elif kind == 3:
+            src, dst, device = buf.at[g, h, 1 - b, second_part(a)], rx2[a].at[n], along_x
+        else:
+            s = step_slab(a, n)
+            src, dst, device = buf.at[g, h, b], rz[a].at[z], (d, r, s)
+            got = (a, z, 4)
+        return remote(src, dst, rsend, rrecv, (a, n, kind), device, got)
+
+    def reduce_one(group, n):
         for a in group:
-            for kind in (1, 2, 3, 4):
-                gather(a, k, kind).wait_send()
-
-    def slot(k):
-        first = (4 - k) // 4
-        return first * SPARE + (1 - first) * flip(z, k - 1 + first)
-
-    def reduce_copy(a, k, kind):
-        buf, g = bufs[a], slot(k)
-        if kind == 0:
-            src, dst, device = buf.at[g, :, 1 - b, first_part(a)], rx[a].at[k], along_x
-        elif kind == 1:
-            src, dst, device = buf.at[g, 1 - h, :, second_part(a)], ry[a].at[k], along_y
-        elif kind == 2:
-            src, dst, device = buf.at[g, 1 - h, b, first_part(a)], ry2[a].at[k], along_y
-        elif kind == 3:
-            src, dst, device = buf.at[g, h, 1 - b, second_part(a)], rx2[a].at[k], along_x
-        else:
-            src, dst, device = buf.at[g, h, b], rz[a].at[k], along_z(k)
-        return remote(src, dst, rsend, rrecv, (a, k, kind), device)
-
-    def reduce_one(group, k):
-        for a in group:
-            reduce_copy(a, k, 0).start()
-            reduce_copy(a, k, 1).start()
+            reduce_copy(a, n, 0).start()
+            reduce_copy(a, n, 1).start()
 
     def scratch(a, place):
-        if a == 0:
-            return tmpq.at[place]
-        return tmp.at[place + (2 if a == 3 else 0)]
-
-    def reduce_two(group, k):
+        return tmp.at[place + (2 if a % 2 else 0)]
+
+    def reduce_two(group, n):
         loads = []
         for a in group:
-            reduce_copy(a, k, 0).wait_recv()
-            reduce_copy(a, k, 1).wait_recv()
+            reduce_copy(a, n, 0).wait_recv()
+            reduce_copy(a, n, 1).wait_recv()
             for place, got in enumerate((rx[a], ry[a])):
                 to = scratch(a, place).at[:, pl.ds(0, parts[a][place])]
-                loads.append(pltpu.make_async_copy(got.at[k], to, local.at[a * 2 + place]))
+                loads.append(pltpu.make_async_copy(got.at[n], to, local.at[a * 2 + place]))
                 loads[-1].start()
-        g = slot(k)
         for i, a in enumerate(group):
+            g = slot(a, n)
             first, second = parts[a]
             loads[2 * i].wait()
             for side in range(2):
                 add_low(bufs[a], (g, side, b, first_part(a)), scratch(a, 0)[side, :first])
-            reduce_copy(a, k, 2).start()
+            reduce_copy(a, n, 2).start()
             loads[2 * i + 1].wait()
             for side in range(2):
                 add_low(bufs[a], (g, h, side, second_part(a)), scratch(a, 1)[side, :second])
-            reduce_copy(a, k, 3).start()
-
-    def reduce_three(group, k):
+            reduce_copy(a, n, 3).start()
+
+    def reduce_three(group, n):
         loads = []
         for a in group:
-            reduce_copy(a, k, 2).wait_recv()
-            reduce_copy(a, k, 3).wait_recv()
+            reduce_copy(a, n, 2).wait_recv()
+            reduce_copy(a, n, 3).wait_recv()
             for place, got in enumerate((ry2[a], rx2[a])):
                 to = scratch(a, place).at[0, pl.ds(0, parts[a][place])]
-                loads.append(pltpu.make_async_copy(got.at[k], to, local.at[a * 2 + place]))
+                loads.append(pltpu.make_async_copy(got.at[n], to, local.at[a * 2 + place]))
                 loads[-1].start()
-        g = slot(k)
         for i, a in enumerate(group):
+            g = slot(a, n)
             first, second = parts[a]
             loads[2 * i].wait()
             add_low(bufs[a], (g, h, b, first_part(a)), scratch(a, 0)[0, :first])
             loads[2 * i + 1].wait()
             add_low(bufs[a], (g, h, b, second_part(a)), scratch(a, 1)[0, :second])
 
-            @pl.when(k > 0)
+            @pl.when(step_slab(a, n) != z)
             def _():
-                reduce_copy(a, k, 4).start()
+                reduce_copy(a, n, 4).start()
 
     def reduce_four(group):
         for a in group:
             rows = bufs[a].shape[3]
-            hold = gqkv if a == 0 else act
             loads = []
             for k in (1, 2, 3):
-                got = remote(bufs[a].at[slot(k), h, b], rz[a].at[k], rsend, rrecv, (a, k, 4), along_z(k))
-                got.wait_recv()
-                loads.append(
-                    pltpu.make_async_copy(rz[a].at[k], hold.at[pl.ds((k - 1) * rows, rows)], local.at[k])
-                )
+                other = flip(z, k)
+                at = rz[a].at[other]
+                remote(at, at, rsend, rrecv, (a, k, 4), along_z(k), (a, other, 4)).wait_recv()
+                loads.append(pltpu.make_async_copy(at, act.at[pl.ds((k - 1) * rows, rows)], local.at[k]))
                 loads[-1].start()
             for load in loads:
                 load.wait()
-            value = bufs[a][SPARE, h, b].astype(F32)
+            value = bufs[a][slot(a, 0 if a in mlp else 3), h, b].astype(F32)
             for k in range(3):
-                value = value + hold[k * rows : (k + 1) * rows].astype(F32)
-            bufs[a][3 - z, h, b] = value.astype(BF)
+                value = value + act[k * rows : (k + 1) * rows].astype(F32)
+            bufs[a][last_slab(a), h, b] = value.astype(BF)
             spread(a, 1).start()
             spread(a, 2).start()
 
@@ -439,35 +478,75 @@
             spread(a, 2, True).wait_recv()
             spread(a, 4).start()
 
+    def qkv_pieces(matrix, side, flat):
+        rows = flat.shape[1]
+        part = matrix.shape[2]
+        cut = rows - part
+        return (
+            (matrix.at[0, side], flat.at[0, pl.ds(0, part)]),
+            (matrix.at[1, side, pl.ds(0, cut)], flat.at[0, pl.ds(part, cut)]),
+            (matrix.at[1, side, pl.ds(cut, part - cut)], flat.at[1, pl.ds(0, part - cut)]),
+            (matrix.at[2, side], flat.at[1, pl.ds(part - cut, part)]),
+        )
+
     def swap_out(a):
-        return remote(bufs[a].at[3 - z, 1 - r], outs[a].at[r], fsend, frecv, (a, 0), partner)
+        mine = bufs[a].at[last_slab(a), 1 - r]
+        if a == 0:
+            pairs = qkv_pieces(outs[a], r, mine)
+            return [remote(src, dst, qsend, qrecv, 4 + i, partner) for i, (dst, src) in enumerate(pairs)]
+        to = outs[a].at[:, :, half_lanes(r)] if a == 2 else outs[a].at[r]
+        return [remote(mine, to, fsend, frecv, (a, 0), partner)]
 
     def keep_out(a):
-        return pltpu.make_async_copy(bufs[a].at[3 - z, r], outs[a].at[r], local.at[a])
+        mine = bufs[a].at[last_slab(a), r]
+        if a == 0:
+            pairs = qkv_pieces(outs[a], r, mine)
+            return [pltpu.make_async_copy(src, dst, qlocal.at[i]) for i, (dst, src) in enumerate(pairs)]
+        to = outs[a].at[:, :, half_lanes(r)] if a == 2 else outs[a].at[r]
+        return [pltpu.make_async_copy(mine, to, local.at[a])]
 
     def reduce_six(group):
         for a in group:
             spread(a, 3, True).wait_recv()
             spread(a, 4, True).wait_recv()
-            swap_out(a).start()
-            keep_out(a).start()
+            for copy in swap_out(a) + keep_out(a):
+                copy.start()
+
+    def half_lanes(side):
+        return pl.ds(pl.multiple_of(side * half, half), half)
 
     def exchange(index, src, dst):
         return remote(src, dst, csend, crecv, index, partner)
 
     rows_own, rows_other = pl.ds(0, own), pl.ds(own, own)
-    sources = (
-        lambda side: qkv_src.at[side],
-        lambda side: proj_src.at[side],
-        lambda side: expand_src.at[:, :, pl.ds(pl.multiple_of(side * half, half), half)],
-        lambda side: shrink_src.at[side],
-    )
+    def source(a, side):
+        if a == 2:
+            return expand_src.at[:, :, half_lanes(side)]
+        return (qkv_src, proj_src, expand_src, shrink_src)[a].at[side]
 
     def source_swap(a):
-        return exchange(a, sources[a](1 - r), bufs[a].at[z, r])
+        to = bufs[a].at[z, r]
+        if a == 0:
+            pairs = qkv_pieces(qkv_src, 1 - r, to)
+            return [remote(src, dst, qsend, qrecv, i, partner) for i, (src, dst) in enumerate(pairs)]
+        return [exchange(a, source(a, 1 - r), to)]
 
     def source_keep(a):
-        return pltpu.make_async_copy(sources[a](r), bufs[a].at[z, r], local.at[a])
+        to = bufs[a].at[z, r]
+        if a == 0:
+            pairs = qkv_pieces(qkv_src, r, to)
+            return [pltpu.make_async_copy(src, dst, qlocal.at[i]) for i, (src, dst) in enumerate(pairs)]
+        return [pltpu.make_async_copy(source(a, r), to, local.at[a])]
+
+    def start_source(group):
+        for a in group:
+            for copy in source_swap(a) + source_keep(a):
+                copy.start()
+
+    def finish_source(group):
+        for a in group:
+            for copy in source_swap(a) + source_keep(a):
+                copy.wait()
 
     grad_load = pltpu.make_async_copy(out_grad, gm.at[rows_own], local.at[4])
     swap_grad = exchange(4, out_grad, gm.at[rows_other])
@@ -489,25 +568,30 @@
         pl.semaphore_signal(barrier, inc=1, device_id=peer, device_id_type=MESH_ID)
     pl.semaphore_wait(barrier, len(peers))
 
-    for a in range(4):
-        source_swap(a).start()
-        source_keep(a).start()
-    bias_load = pltpu.make_async_copy(biases, bias_all.at[z], local.at[5])
-    bias_load.start()
+    start_source(attn)
     grad_load.start()
-    swap_grad.start()
-    bias_load.wait()
+    bias_all[z] = jnp.zeros(bias_all.shape[1:], F32)
+    part = qkv_bias_in.shape[1] // 2
+    for side in range(2):
+
+        @pl.when(r == side)
+        def _():
+            bias_all[z, 0:1, :half] = expand_bias_in[side * half : (side + 1) * half].reshape(1, half)
+            for i in range(2):
+                at = half + 2 * i * part
+                bias_all[z, 0:1, at : at + part] = qkv_bias_in[i : i + 1, side * part : (side + 1) * part]
+
+    finish_source(attn)
+    start_z(attn)
     for k in (1, 2, 3):
         bias_copy(k).start()
-    for a in attn:
-        source_swap(a).wait()
-        source_keep(a).wait()
-    for k in (1, 2, 3):
-        start_z(attn, k)
-
-    gain_one, shift_one = vectors[0:1, :], vectors[1:2, :]
-    gain_two, shift_two = vectors[2:3, :], vectors[3:4, :]
-    proj_bias, shrink_bias = vectors[4:5, :], vectors[5:6, :]
+
+    def as_row(ref):
+        return ref[...].reshape(1, width)
+
+    gain_one, shift_one, gain_two, shift_two, proj_bias, shrink_bias = (
+        as_row(ref) for ref in (gain_one_in, shift_one_in, gain_two_in, shift_two_in, proj_bias_in, shrink_bias_in)
+    )
 
     def over_rows(body):
         @pl.loop(0, own // CHUNK)
@@ -540,46 +624,48 @@
 
     over_rows(first_rows)
     swap_h1.start()
+    start_source(mlp)
+    swap_grad.start()
+    rel_pad[...] = jnp.zeros_like(rel_pad)
+    rel_pad[0, : rel_h_in.shape[0]] = rel_h_in[...]
+    rel_pad[1, : rel_w_in.shape[0]] = rel_w_in[...]
+    relative_tables(rel_pad.at[0], rel_pad.at[1], rel_query, rel_back)
     total[...] = jnp.zeros_like(total)
-    for k in (1, 2, 3):
-        bias_copy(k, True).wait_recv()
     swap_h1.wait_recv()
 
     def bias_q_of(s):
-        return bias_all[s, 0:1, half : half + wq.shape[4]]
+        return bias_all[s, 0:1, half : half + gqkv.shape[1]]
 
     def bias_e_of(s):
         return bias_all[s, 0:1, :half]
 
     @pl.loop(0, 4)
-    def _(k):
-        s = flip(z, k)
-
-        @pl.when(k > 0)
-        def _():
-            pass_diagonal(attn, k)
-            finish_slab(attn, k)
-
+    def _(i):
+        @pl.when(i == 1)
+        def _():
+            for k in (1, 2, 3):
+                bias_copy(k, True).wait_recv()
+            for n in (1, 2, 3):
+                arrive(attn, n)
+            finish_source(mlp)
+            start_z((3, 2))
+            for n in (1, 2, 3):
+                pass_diagonal(attn, n)
+
+        @pl.when(i > 0)
+        def _():
+            finish_slab(attn, i)
+
+        s = slab_of(i)
         attention_slab(
             s, h1, wq, wp, bias_q_of(s), rel_query, codes, attended, total, heads, half
         )
 
-        @pl.when(k == 0)
-        def _():
-            pass_xy(attn, 1)
-            for a in mlp:
-                source_swap(a).wait()
-                source_keep(a).wait()
-            start_z(mlp, 1)
-
-        @pl.when(k < 2)
-        def _():
-            pass_xy(attn, k + 2)
-            start_z(mlp, k + 2)
-
-        @pl.when(k >= 2)
-        def _():
-            pass_xy(mlp, k - 1)
+    arrive(shrink, 1)
+
+    @pl.when(is_inner)
+    def _():
+        arrive(shrink, 2)
 
     swap_attn.start()
     swap_attn.wait()
@@ -607,51 +693,68 @@
     swap_h2.wait()
 
     @pl.loop(0, 4)
-    def _(k):
-        s = flip(z, k)
-        g = slot(k)
-
-        @pl.when(k > 0)
-        def _():
-            finish_slab(mlp, k)
+    def _(n):
+        s = slab_of(n)
+        g = slot(2, n)
+
+        @pl.when(n > 0)
+        def _():
+            finish_slab(shrink, n)
 
         mlp_rows(s, 0, h2, gm, we, ws, bias_e_of(s), act, gpre, total, back, bias_e, half)
 
-        @pl.when(k < 3)
-        def _():
-            pass_diagonal(mlp, k + 1)
+        @pl.when(n == 0)
+        def _():
+            arrive(whole, 1)
+            pass_diagonal(shrink, 1)
+
+            @pl.when(is_inner)
+            def _():
+                arrive(whole, 2)
+                pass_diagonal(shrink, 2)
+
+        @pl.when((n == 1) | ((n == 2) & is_end))
+        def _():
+            arrive(shrink, n + 1 + (z + 1) // 2 % 2)
 
         mlp_rows(s, 1, h2, gm, we, ws, bias_e_of(s), act, gpre, total, back, bias_e, half)
 
-        @pl.when(k == 1)
-        def _():
-            sent_z(mlp)
-
-        @pl.when(k > 1)
-        def _():
-            sent_xy(mlp, k - 1)
-
-        @pl.when(k == 3)
-        def _():
-            sent_xy(mlp, 3)
+        @pl.when(n > 0)
+        def _():
+            sent_slab(mlp, n - 1)
+
+        @pl.when(n == 3)
+        def _():
+            sent_slab(mlp, 3)
 
         for side in range(2):
             columns = slice(side * half, side * half + half)
             we[g, side] = dot_tn(h2[:, columns], gpre[...]).astype(BF).reshape(we.shape[2:])
             ws[g, side] = dot_tn(act[: 2 * own], gm[:, columns]).astype(BF).reshape(ws.shape[2:])
-        reduce_one(mlp, k)
-
-        @pl.when(k == 1)
-        def _():
-            pass_xy(mlp, 3)
-
-        @pl.when(k > 0)
-        def _():
-            reduce_two(mlp, k - 1)
+
+        more = (n == 1) | ((n == 2) & is_end)
+
+        @pl.when(more)
+        def _():
+            pass_diagonal(shrink, n + 1 + (z + 1) // 2 % 2)
+
+        reduce_one(mlp, n)
+
+        @pl.when(n > 0)
+        def _():
+            reduce_two(mlp, n - 1)
+
+        @pl.when(n > 1)
+        def _():
+            reduce_three(mlp, n - 2)
+
+        @pl.when(more)
+        def _():
+            arrive(whole, n + 1 + (z + 1) // 2 % 2)
 
     swap_mlp.start()
     swap_gh2.start()
-    reduce_two(mlp, 3)
+    reduce_three(mlp, 2)
     swap_mlp.wait()
     swap_gh2.wait()
 
@@ -682,40 +785,40 @@
     back[...] = jnp.zeros_like(back)
     swap_ga.wait()
 
+    reduce_two(mlp, 3)
+    for i in range(4):
+        sent_slab(attn, i)
+
     @pl.loop(0, 4)
-    def _(k):
-        s = flip(z, k)
-        g = slot(k)
+    def _(n):
+        s = slab_of(3 - n)
+        g = slot(0, n)
         attention_back_slab(
             s, h1, gm, wq, wp, bias_q_of(s), rel_query, rel_back, codes, gqkv, back, bias_q, rel_acc, heads, half
         )
-
-        @pl.when(k == 1)
-        def _():
-            sent_z(attn)
-
-        @pl.when(k > 1)
-        def _():
-            sent_xy(attn, k - 1)
-
-        @pl.when(k == 3)
-        def _():
-            sent_xy(attn, 3)
-
         for side in range(2):
             columns = slice(side * half, side * half + half)
-            wq[g, side] = dot_tn(h1[:, columns], gqkv[: 2 * own]).astype(BF).reshape(wq.shape[2:])
+            wq[g, side] = dot_tn(gqkv[...], h1[:, columns]).astype(BF).reshape(wq.shape[2:])
             wp[g, side] = dot_tn(attended[s], gm[:, columns]).astype(BF).reshape(wp.shape[2:])
-        reduce_one(attn, k)
-        reduce_three(mlp, k)
-
-        @pl.when(k > 0)
-        def _():
-            reduce_two(attn, k - 1)
+        reduce_one(attn, n)
+
+        @pl.when(n == 0)
+        def _():
+            reduce_three(mlp, 3)
+
+        @pl.when(n > 0)
+        def _():
+            reduce_two(attn, n - 1)
+
+        @pl.when(n > 1)
+        def _():
+            reduce_three(attn, n - 2)
 
     swap_gh1.start()
+    reduce_four((2,))
+    reduce_three(attn, 2)
     reduce_two(attn, 3)
-    reduce_four(mlp)
+    reduce_four((3,))
     swap_gh1.wait()
 
     def input_rows(rows):
@@ -756,22 +859,19 @@
         return finish
 
     finish = small_step(0, partner)
-    reduce_three(attn, 0)
+    reduce_three(attn, 3)
     finish()
     finish = small_step(1, along_x)
-    reduce_three(attn, 1)
-    reduce_three(attn, 2)
+    reduce_four(attn)
     finish()
     finish = small_step(2, along_y)
-    reduce_three(attn, 3)
     reduce_five(mlp)
     finish()
     finish = small_step(3, along_z(1))
-    reduce_four(attn)
+    reduce_five(attn)
     finish()
     finish = small_step(4, along_z(2))
     reduce_six(mlp)
-    reduce_five(attn)
     finish()
     small_store = pltpu.make_async_copy(small, small_out, local.at[6])
     rel_store = pltpu.make_async_copy(rel, rel_out, local.at[7])
@@ -783,66 +883,68 @@
     for k in (1, 2, 3):
         bias_copy(k).wait_send()
     for a in range(4):
-        swap_out(a).wait()
-        keep_out(a).wait()
+        for copy in swap_out(a) + keep_out(a):
+            copy.wait()
         for kind in (1, 2, 3, 4):
             spread(a, kind).wait_send()
-        for k in range(4):
+        for n in range(4):
             for kind in range(4):
-                reduce_copy(a, k, kind).wait_send()
-            if k > 0:
-                reduce_copy(a, k, 4).wait_send()
+                reduce_copy(a, n, kind).wait_send()
+
+            @pl.when(step_slab(a, n) != z)
+            def _():
+                reduce_copy(a, n, 4).wait_send()
+
     small_store.wait()
     rel_store.wait()
     result_store.wait()
     input_store.wait()
 
 
-def run_kernel(
-    tokens, keep, out_grad, vectors, biases, codes, rel_query, rel_back, qkv_src, proj_src, expand_src, shrink_src
-):
+def run_kernel(tokens, keep, out_grad, vectors, qkv_bias, expand_bias, rel_height, rel_width, sources):
     own, width = tokens.shape
-    sources = (qkv_src, proj_src, expand_src, shrink_src)
-    rows = [qkv_src.shape[2], proj_src.shape[2], expand_src.shape[1], shrink_src.shape[2]]
-    lanes = [qkv_src.shape[3], proj_src.shape[3], width // 2, shrink_src.shape[3]]
+    half = width // 2
+    rows = [source.shape[-2] for source in sources]
+    rows[0] = 3 * rows[0] // 2
     sds = jax.ShapeDtypeStruct
     any_spec = pl.BlockSpec(memory_space=pl.ANY)
     vmem_spec = pl.BlockSpec(memory_space=pltpu.VMEM)
     out_shape = [sds((own, width), BF), sds((own, width), F32)]
-    out_shape += [sds((2, 2, n, l), BF) for n, l in zip(rows, lanes)]
+    out_shape += [sds(source.shape, BF) for source in sources]
     out_shape += [sds((SMALL_ROWS, width), F32), sds((LANES, LANES), F32)]
     first, second = zip(*[halves(n) for n in rows])
-    out_shape += [sds((4, 2, n, l), BF) for n, l in zip(first, lanes)]
-    out_shape += [sds((4, 2, n, l), BF) for n, l in zip(second, lanes)]
-    out_shape += [sds((4, n, l), BF) for n, l in zip(second, lanes)]
-    out_shape += [sds((4, n, l), BF) for n, l in zip(first, lanes)]
-    out_shape += [sds((4, n, l), BF) for n, l in zip(rows, lanes)]
+    out_shape += [sds((4, 2, n, half), BF) for n in first]
+    out_shape += [sds((4, 2, n, half), BF) for n in second]
+    out_shape += [sds((4, n, half), BF) for n in second]
+    out_shape += [sds((4, n, half), BF) for n in first]
+    out_shape += [sds((4, n, half), BF) for n in rows]
     both = 2 * own
     vmem, dma = pltpu.VMEM, pltpu.SemaphoreType.DMA
-    hidden, qkv_width = lanes[3], lanes[0]
-    scratch = [vmem((5, 2, 2, n, l), BF) for n, l in zip(rows, lanes)]
+    qkv_width = 2 * rows[0]
+    scratch = [vmem((5, 2, 2, n, half), BF) for n in rows]
     scratch += [vmem((both, width), BF)] * 3
     scratch += [vmem((4, both, qkv_width // 3), BF)]
     scratch += [vmem((both, width), F32)] * 2
     scratch += [vmem((own, width), F32)] * 3
-    deep = max(both, 3 * rows[2])
-    scratch += [vmem((deep, hidden), BF), vmem((both, hidden), BF), vmem((deep, qkv_width), BF)]
-    scratch += [vmem((4, 2, first[2], hidden), BF), vmem((2, 2, first[0], qkv_width), BF)]
+    scratch += [vmem((max(both, 3 * rows[2]), half), BF), vmem((both, half), BF), vmem((both, qkv_width), BF)]
+    scratch += [vmem((4, 2, first[2], half), BF)]
     scratch += [vmem((4, 8, width), F32), vmem((SMALL_ROWS, width), F32), vmem((5, SMALL_ROWS, width), F32)]
     scratch += [vmem((LANES, LANES), F32), vmem((5, LANES, LANES), F32)]
-    scratch += [vmem((4, 1, hidden), F32), vmem((4, 1, qkv_width), F32), vmem((2 * LANES, LANES), F32)]
-    scratch += [dma((4, 4, 5))] * 4 + [dma((4, 5))] * 2 + [dma((22,))] * 2 + [dma((4,))] * 2 + [dma((10,))]
+    scratch += [vmem((4, 1, half), F32), vmem((4, 1, qkv_width), F32), vmem((2 * LANES, LANES), F32)]
+    scratch += [vmem((2 * LANES, LANES), BF), vmem((3 * LANES, LANES), BF), vmem((2, 32, HEAD), F32)]
+    scratch += [dma((4, 4, 6))] * 2 + [dma((4, 4, 5))] * 2 + [dma((4, 5))] * 2 + [dma((22,))] * 2
+    scratch += [dma((4,))] * 2 + [dma((8,))] * 2 + [dma((10,)), dma((4,))]
     got = pl.pallas_call(
         kernel,
         out_shape=out_shape,
-        in_specs=[vmem_spec, vmem_spec, any_spec, vmem_spec, any_spec] + [vmem_spec] * 3 + [any_spec] * 4,
+        in_specs=[vmem_spec, vmem_spec, any_spec] + [vmem_spec] * 11 + [any_spec] * 4,
         out_specs=[any_spec] * len(out_shape),
         scratch_shapes=scratch,
         compiler_params=pltpu.CompilerParams(
             collective_id=0, has_side_effects=True, vmem_limit_bytes=VMEM_LIMIT
         ),
         name="block_step",
-    )(tokens, keep, out_grad, vectors, biases, codes, rel_query, rel_back, *sources)
+    )(tokens, keep, out_grad, *vectors, qkv_bias, expand_bias, rel_height, rel_width, key_codes(), *sources)
     return got[:8]
 
 
@@ -856,7 +958,6 @@
     windows, per, width = tokens.shape
     side = (rel_height.shape[0] + 1) // 2
     count, head = rel_height.shape
-    r = lax.axis_index("row")
 
     def padded(value):
         grid = value.reshape(windows, side, side, -1)
@@ -870,29 +971,21 @@
     rows, _, local_width = qkv_weight.shape
     part = local_width // 2
     hidden = expand_weight.shape[1] // 2
-    qkv_src = qkv_weight.reshape(rows, 3, 2, part).transpose(2, 0, 1, 3).reshape(2, 2, rows // 2, 3 * part)
+    qkv_src = qkv_weight.transpose(1, 2, 0).reshape(3, 2, part, rows)
     proj_src = proj_weight.reshape(2, 2, part // 2, proj_weight.shape[1])
     expand_src = expand_weight.reshape(2, rows // 2, 2 * hidden)
     shrink_src = shrink_weight.reshape(2, 2, hidden // 2, shrink_weight.shape[1])
-    zeros = jnp.zeros((part,), F32)
-    query_bias, value_bias = (lax.dynamic_slice_in_dim(qkv_bias[i], r * part, part) for i in range(2))
-    bias = jnp.concatenate(
-        [lax.dynamic_slice_in_dim(expand_bias, r * hidden, hidden), query_bias, zeros, value_bias]
-    )
-    biases = jnp.pad(bias[None], ((0, 7), (0, width - bias.shape[0])))
-    vectors = jnp.stack([first_gain, first_shift, second_gain, second_shift, proj_bias, shrink_bias])
-    vectors = jnp.pad(vectors, ((0, 2), (0, 0)))
-    rel_query, rel_back = relative_tables(rel_height, rel_width)
+    vectors = (first_gain, first_shift, second_gain, second_shift, proj_bias, shrink_bias)
     keep = padded(valid_mask.astype(F32))
     got = run_kernel(
-        padded(tokens), keep, padded(out_grad), vectors, biases, key_codes(), rel_query, rel_back,
-        qkv_src, proj_src, expand_src, shrink_src,
+        padded(tokens), keep, padded(out_grad), vectors, qkv_bias, expand_bias, rel_height, rel_width,
+        (qkv_src, proj_src, expand_src, shrink_src),
     )
     block_low, grad, qkv_got, proj_got, expand_got, shrink_got, small, rel = got
-    qkv_sum = qkv_got.astype(F32).reshape(2, rows, 3, part).transpose(1, 2, 0, 3).reshape(rows, 3, 2 * part)
-    proj_sum = proj_got.astype(F32).reshape(2 * part, -1)
-    expand_sum = expand_got.astype(F32).reshape(2, rows, hidden).transpose(1, 0, 2).reshape(rows, 2 * hidden)
-    shrink_sum = shrink_got.astype(F32).reshape(2 * hidden, -1)
+    qkv_sum = qkv_got.astype(F32).reshape(3, local_width, rows).transpose(2, 0, 1)
+    proj_sum = proj_got.astype(F32).reshape(proj_weight.shape)
+    expand_sum = expand_got.astype(F32).reshape(expand_weight.shape)
+    shrink_sum = shrink_got.astype(F32).reshape(shrink_weight.shape)
     rms = jnp.sqrt(jnp.sum(small[:5], axis=1) / (small[5, 0] * width))
     slabs = small[SMALL_ROWS - 8 :].reshape(2, 4, width)
     mine = lax.dynamic_index_in_dim(slabs, lax.axis_index("col"), axis=1, keepdims=False)

time: 509 us -> 405 us (0.80)
  Pallas kernels: 447 us -> 375 us
  local copies, waits for them, and re-layouts: 47.6 us -> 17.8 us
    pallas_call x1, Pallas kernels: 447 us -> 375 us  [run_kernel(): pl.pallas_call(kernel, out_shape=out_shape, in_specs=[vmem_spec, vmem_spe...]
    reshape x7 -> x0, local copies, waits for them, and re-layouts: 17.2 us -> none  [the longest x3 10.4 us: over_chips(): qkv_got.astype(F32).reshape(2, rows, 3, part).transpose(1, 2, 0, 3)]
where the time goes in v2:
time: 405 us; the launch traced here: 404 us
  Pallas kernels  375 us (93%)
  local copies, waits for them, and re-layouts  17.8 us (4%)
  other arithmetic  9.64 us (2%)
    pallas_call x1, Pallas kernels, run_kernel(): pl.pallas_call(kernel, out_shape=out_shape, in_specs=[vmem_spec, vmem_spe...  375 us

profile of v2, /device:TPU:0, one launch (start us, length us, event | category | flops | bytes accessed | tf_op | source)
XLA Modules:
  0.0 403.9 jit_solution(666235140089011492)
XLA Ops:
  0.7 1.3 copy.44
  2.0 0.0 copy-start.4
  2.0 1.1 pad.11
  3.1 0.5 copy-done.4
  3.6 0.1 copy.45
  3.7 0.0 copy-start.6
  3.8 1.1 pad.13
  4.9 0.0 copy-done.6
  4.9 0.1 reshape.114
  5.0 0.8 reshape.144.keep
  5.8 375.1 %block_step.1 = (bf16[448,1280]{1,0:T(8,128)(2,1)}, f32[448,1280]{1,0:T(8,128)}, bf16[3,2,160,640]{3,2,1,0:T(8,128)(2,1)}, bf16[2,2,80,640]{3,2,1,0:T(8,128)(2,1...) custom-call(bf16[448,1280]{1,0:T(8,128)(2,1)} %bitcast.37, ...), custom_call_target="tpu_custom_call" | custom-call | tf_op jit(solution)/shard_map/block_step/pallas_call | solution.py:937
  380.9 1.2 slice.63
  382.7 0.9 slice_reduce_fusion
  383.6 0.5 divide_sqrt_fusion
  384.2 0.8 slice.52
  385.0 0.1 reshape.128
  385.1 0.7 reshape.129
  385.8 0.6 reshape.134
  386.4 1.7 slice_reduce_fusion.1
  388.1 1.3 fusion
  389.4 0.6 rev.3
  390.0 0.0 copy-start.1
  390.0 3.5 bitcast_convert_fusion
  393.5 0.0 copy-done.1
  393.5 0.0 copy-start.2
  393.5 2.1 bitcast_convert_fusion.1
  395.6 0.0 copy-done.2
  395.6 0.0 copy-start
  395.6 1.7 convert_bitcast_fusion
  397.3 0.8 copy-done
  398.1 0.0 copy-start.3
  398.1 2.8 copy.48
  400.9 0.0 copy-start.5
  401.0 0.0 copy-done.3
  401.0 2.0 copy.47
  402.9 0.0 copy-done.5
  402.9 1.0 bitcast_convert_fusion.2
  (9 shorter events, 0.1 us)
Async XLA Ops:
  2.0 1.6 copy-start.4
  3.7 1.1 copy-start.6
  390.0 3.5 copy-start.1
  393.5 2.1 copy-start.2
  395.6 2.5 copy-start
  398.1 2.8 copy-start.3
  400.9 2.0 copy-start.5

commit v3 on v2

--- a/solution.py
+++ b/solution.py
@@ -200,11 +200,13 @@
 
 
 def attention_back_slab(
-    s, h1, ga, wq, wp, bias, rel_query, rel_back, codes, gqkv, back, bias_grad, rel_grad, heads, half
+    s, first, h1, ga, wq, wp, bias, rel_query, rel_back, codes, gqkv, back, bias_grad, rel_grad, heads, half
 ):
-    @pl.loop(0, h1.shape[0] // WROWS)
+    count = h1.shape[0] // WROWS // 2
+
+    @pl.loop(0, count)
     def _(m):
-        rows = pl.ds(pl.multiple_of(m * WROWS, WROWS), WROWS)
+        rows = pl.ds(pl.multiple_of((first * count + m) * WROWS, WROWS), WROWS)
         low = qkv_low(s, rows, h1, wq, bias, half)
         grad = (dot_nt(ga[rows, :half], block(wp, s, 0)) + dot_nt(ga[rows, half:], block(wp, s, 1))).astype(BF)
         parts = [[], [], []]
@@ -227,7 +229,6 @@
 ARRAYS = ("qkv", "proj", "expand", "shrink")
 CHUNK = 64
 EPS = 1e-06
-SMALL_ROWS = 24
 SPARE = 4
 
 
@@ -252,10 +253,10 @@
 def kernel(
     tokens, keep, out_grad, gain_one_in, shift_one_in, gain_two_in, shift_two_in, proj_bias_in, shrink_bias_in,
     qkv_bias_in, expand_bias_in, rel_h_in, rel_w_in, codes, qkv_src, proj_src, expand_src, shrink_src,
-    block_out, input_grad, qkv_out, proj_out, expand_out, shrink_out, small_out, rel_out,
+    block_out, input_grad, qkv_out, proj_out, expand_out, shrink_out, early_out, late_out, rel_out,
     rxq, rxp, rxe, rxs, ryq, ryp, rye, rys, rx2q, rx2p, rx2e, rx2s, ry2q, ry2p, ry2e, ry2s, rzq, rzp, rze, rzs,
     wq, wp, we, ws, h1, gm, h2, attended, total, back, xr, xr2, middle, act, gpre, gqkv, tmp,
-    bias_all, small, small_got, rel, rel_got, bias_e, bias_q, rel_acc, rel_query, rel_back, rel_pad,
+    bias_all, early, early_got, late, late_got, rel, rel_got, bias_e, bias_q, rel_acc, rel_query, rel_back, rel_pad,
     gsend, grecv, rsend, rrecv, fsend, frecv, csend, crecv, zsend, zrecv, qsend, qrecv, local, qlocal,
 ):
     d, r, z = lax.axis_index("dp"), lax.axis_index("row"), lax.axis_index("col")
@@ -274,6 +275,7 @@
 
     along_x = (h * 2 + 1 - b, r, z)
     along_y = ((1 - h) * 2 + b, r, z)
+    across = ((1 - h) * 2 + 1 - b, r, z)
     partner = (d, 1 - r, z)
 
     def along_z(k):
@@ -341,14 +343,17 @@
     def start_z(group):
         sends_along_z(group, z, lambda copy: copy.start())
 
-    def arrive(group, i):
+    def relay(group, i):
         s = slab_of(i)
         for a in group:
             gather_z(a, s, 1).wait_recv()
             sends_along_z((a,), s, lambda copy: copy.start())
-            if a not in whole:
-                gather(a, s, 1).start()
-                gather(a, s, 2).start()
+
+    def share(group, i):
+        s = slab_of(i)
+        for a in group:
+            gather(a, s, 1).start()
+            gather(a, s, 2).start()
 
     def pass_diagonal(group, i):
         s = slab_of(i)
@@ -375,8 +380,11 @@
                     for kind in (1, 2, 3, 4):
                         gather(a, s, kind).wait_send()
 
+    def arrival(a, n):
+        return n if a in mlp else 3 - n
+
     def step_slab(a, n):
-        return slab_of(n if a in mlp else 3 - n)
+        return slab_of(arrival(a, n))
 
     def last_slab(a):
         return step_slab(a, 3)
@@ -396,11 +404,26 @@
             src, dst, device = buf.at[g, 1 - h, b, first_part(a)], ry2[a].at[n], along_y
         elif kind == 3:
             src, dst, device = buf.at[g, h, 1 - b, second_part(a)], rx2[a].at[n], along_x
-        else:
+        elif kind == 4:
             s = step_slab(a, n)
             src, dst, device = buf.at[g, h, b], rz[a].at[z], (d, r, s)
             got = (a, z, 4)
-        return remote(src, dst, rsend, rrecv, (a, n, kind), device, got)
+        else:
+            i = arrival(a, n)
+            src, dst, device = buf.at[g, h, b], rz[a].at[2 + i], (d, r, slab_of(1))
+            got = (a, i, 5)
+        return remote(src, dst, rsend, rrecv, (a, n, min(kind, 4)), device, got)
+
+    def reduce_z(a, n, act_on):
+        i = arrival(a, n)
+
+        @pl.when((i > 0) & (is_inner | (i == 1)))
+        def _():
+            act_on(reduce_copy(a, n, 4))
+
+        @pl.when(is_end & (i > 1))
+        def _():
+            act_on(reduce_copy(a, n, 5))
 
     def reduce_one(group, n):
         for a in group:
@@ -448,24 +471,39 @@
             loads[2 * i + 1].wait()
             add_low(bufs[a], (g, h, b, second_part(a)), scratch(a, 1)[0, :second])
 
-            @pl.when(step_slab(a, n) != z)
+            i = arrival(a, n)
+
+            @pl.when(is_inner & (i > 1))
             def _():
-                reduce_copy(a, n, 4).start()
+                at = rz[a].at[2 + i]
+                remote(at, at, rsend, rrecv, (a, n, 4), (d, r, slab_of(1)), (a, i, 5)).wait_recv()
+                pieces = ((0, first, first_part(a)), (1, second, second_part(a)))
+                copies = [
+                    pltpu.make_async_copy(at.at[part], scratch(a, 0).at[side, pl.ds(0, count)], local.at[a * 2 + side])
+                    for side, count, part in pieces
+                ]
+                for copy in copies:
+                    copy.start()
+                for copy, (side, count, part) in zip(copies, pieces):
+                    copy.wait()
+                    add_low(bufs[a], (g, h, b, part), scratch(a, 0)[side, :count])
+
+            reduce_z(a, n, lambda copy: copy.start())
 
     def reduce_four(group):
         for a in group:
             rows = bufs[a].shape[3]
             loads = []
-            for k in (1, 2, 3):
-                other = flip(z, k)
+            for k in (1, 2):
+                other = slab_of(k)
                 at = rz[a].at[other]
-                remote(at, at, rsend, rrecv, (a, k, 4), along_z(k), (a, other, 4)).wait_recv()
+                remote(at, at, rsend, rrecv, (a, k, 4), (d, r, other), (a, other, 4)).wait_recv()
                 loads.append(pltpu.make_async_copy(at, act.at[pl.ds((k - 1) * rows, rows)], local.at[k]))
                 loads[-1].start()
             for load in loads:
                 load.wait()
             value = bufs[a][slot(a, 0 if a in mlp else 3), h, b].astype(F32)
-            for k in range(3):
+            for k in range(2):
                 value = value + act[k * rows : (k + 1) * rows].astype(F32)
             bufs[a][last_slab(a), h, b] = value.astype(BF)
             spread(a, 1).start()
@@ -563,7 +601,7 @@
         return remote(at, at, zsend, zrecv, k, along_z(k))
 
     barrier = pltpu.get_barrier_semaphore()
-    peers = [partner, along_x, along_y, along_z(1), along_z(2), along_z(3)]
+    peers = [partner, along_x, along_y, across, along_z(1), along_z(2), along_z(3)]
     for peer in peers:
         pl.semaphore_signal(barrier, inc=1, device_id=peer, device_id_type=MESH_ID)
     pl.semaphore_wait(barrier, len(peers))
@@ -585,6 +623,7 @@
     start_z(attn)
     for k in (1, 2, 3):
         bias_copy(k).start()
+    start_source(mlp)
 
     def as_row(ref):
         return ref[...].reshape(1, width)
@@ -612,19 +651,19 @@
         along = jnp.mean(scaled * xhat, axis=1, keepdims=True)
         return (scaled - mean - xhat * along) * inverse
 
-    small[...] = jnp.zeros_like(small)
+    early[...] = jnp.zeros_like(early)
+    late[...] = jnp.zeros_like(late)
 
     def first_rows(rows):
         value = tokens[rows].astype(F32)
         valid = keep[rows]
         xhat, _ = normalize(value)
         h1[rows] = ((xhat * gain_one + shift_one) * valid).astype(BF)
-        small[0:1, :] += column_sum(valid * value * value)
-        small[5:6, :] += jnp.broadcast_to(column_sum(valid), (1, width))
+        early[0:1, :] += column_sum(valid * value * value)
+        early[5:6, :] += jnp.broadcast_to(column_sum(valid), (1, width))
 
     over_rows(first_rows)
     swap_h1.start()
-    start_source(mlp)
     swap_grad.start()
     rel_pad[...] = jnp.zeros_like(rel_pad)
     rel_pad[0, : rel_h_in.shape[0]] = rel_h_in[...]
@@ -639,34 +678,73 @@
     def bias_e_of(s):
         return bias_all[s, 0:1, :half]
 
+    finish_source(mlp)
+
+    @pl.when(is_end)
+    def _():
+        start_z((3, 2))
+
+    relay(attn, 1)
+    share(attn, 1)
+
     @pl.loop(0, 4)
     def _(i):
         @pl.when(i == 1)
         def _():
+            relay(attn, 2)
+            share(attn, 2)
+            relay(attn, 3)
+
+            @pl.when(is_inner)
+            def _():
+                start_z(shrink)
+                relay(shrink, 1)
+
+            pass_diagonal(attn, 1)
+            share(attn, 3)
+            pass_diagonal(attn, 2)
             for k in (1, 2, 3):
                 bias_copy(k, True).wait_recv()
-            for n in (1, 2, 3):
-                arrive(attn, n)
-            finish_source(mlp)
-            start_z((3, 2))
-            for n in (1, 2, 3):
-                pass_diagonal(attn, n)
+
+            @pl.when(is_inner)
+            def _():
+                relay(shrink, 2)
 
         @pl.when(i > 0)
         def _():
             finish_slab(attn, i)
+
+        @pl.when(i == 2)
+        def _():
+            pass_diagonal(attn, 3)
+
+        @pl.when((i == 1) & is_inner)
+        def _():
+            relay(shrink, 3)
+            start_z(whole)
+
+        @pl.when((i > 0) & is_end)
+        def _():
+            relay(shrink, i)
+
+        @pl.when((i == 3) & is_inner)
+        def _():
+            relay(whole, 1)
+
+        @pl.when(i > 0)
+        def _():
+            share(shrink, i)
+
+        @pl.when(i == 3)
+        def _():
+            pass_diagonal(shrink, 1)
 
         s = slab_of(i)
         attention_slab(
             s, h1, wq, wp, bias_q_of(s), rel_query, codes, attended, total, heads, half
         )
 
-    arrive(shrink, 1)
-
-    @pl.when(is_inner)
-    def _():
-        arrive(shrink, 2)
-
+    pass_diagonal(shrink, 2)
     swap_attn.start()
     swap_attn.wait()
 
@@ -678,8 +756,8 @@
         middle[rows] = mid
         xhat, _ = normalize(mid)
         h2[rows] = (xhat * gain_two + shift_two).astype(BF)
-        small[1:2, :] += column_sum(valid * mid * mid)
-        small[3:4, :] += column_sum(valid * attn_out * attn_out)
+        early[1:2, :] += column_sum(valid * mid * mid)
+        early[3:4, :] += column_sum(valid * attn_out * attn_out)
 
     over_rows(middle_rows)
     swap_h2.start()
@@ -701,21 +779,27 @@
         def _():
             finish_slab(shrink, n)
 
+        @pl.when((n > 0) & is_end)
+        def _():
+            relay(whole, n)
+
+        @pl.when((n == 0) & is_inner)
+        def _():
+            relay(whole, 2)
+
+        @pl.when((n > 1) & is_end)
+        def _():
+            reduce_two(mlp, n - 1)
+
         mlp_rows(s, 0, h2, gm, we, ws, bias_e_of(s), act, gpre, total, back, bias_e, half)
 
         @pl.when(n == 0)
         def _():
-            arrive(whole, 1)
-            pass_diagonal(shrink, 1)
-
-            @pl.when(is_inner)
-            def _():
-                arrive(whole, 2)
-                pass_diagonal(shrink, 2)
-
-        @pl.when((n == 1) | ((n == 2) & is_end))
-        def _():
-            arrive(shrink, n + 1 + (z + 1) // 2 % 2)
+            pass_diagonal(shrink, 3)
+
+        @pl.when((n == 1) & is_inner)
+        def _():
+            relay(whole, 3)
 
         mlp_rows(s, 1, h2, gm, we, ws, bias_e_of(s), act, gpre, total, back, bias_e, half)
 
@@ -732,29 +816,27 @@
             we[g, side] = dot_tn(h2[:, columns], gpre[...]).astype(BF).reshape(we.shape[2:])
             ws[g, side] = dot_tn(act[: 2 * own], gm[:, columns]).astype(BF).reshape(ws.shape[2:])
 
-        more = (n == 1) | ((n == 2) & is_end)
-
-        @pl.when(more)
-        def _():
-            pass_diagonal(shrink, n + 1 + (z + 1) // 2 % 2)
-
         reduce_one(mlp, n)
 
-        @pl.when(n > 0)
+        @pl.when(n == 1)
+        def _():
+            reduce_two(mlp, 0)
+
+        @pl.when((n > 1) & is_inner)
         def _():
             reduce_two(mlp, n - 1)
 
-        @pl.when(n > 1)
-        def _():
-            reduce_three(mlp, n - 2)
-
-        @pl.when(more)
-        def _():
-            arrive(whole, n + 1 + (z + 1) // 2 % 2)
+        @pl.when(n == 2)
+        def _():
+            reduce_three(mlp, 0)
+
+        @pl.when((n == 3) | ((n == 2) & is_end))
+        def _():
+            reduce_three(mlp, n - 1 - (z + 1) // 2 % 2)
+
 
     swap_mlp.start()
     swap_gh2.start()
-    reduce_three(mlp, 2)
     swap_mlp.wait()
     swap_gh2.wait()
 
@@ -764,19 +846,19 @@
         mlp_out = total[rows] + xr[rows] + shrink_bias
         result = mid + mlp_out
         h2[rows] = result.astype(BF)
-        small[2:3, :] += column_sum(valid * result * result)
-        small[4:5, :] += column_sum(valid * mlp_out * mlp_out)
+        early[2:3, :] += column_sum(valid * result * result)
+        early[4:5, :] += column_sum(valid * mlp_out * mlp_out)
         grad_out = gm[rows].astype(F32)
-        small[11:12, :] += column_sum(grad_out)
+        early[9:10, :] += column_sum(grad_out)
         grad = back[rows] + xr2[rows]
         xhat, inverse = normalize(mid)
-        small[8:9, :] += column_sum(grad * xhat)
-        small[9:10, :] += column_sum(grad)
+        early[6:7, :] += column_sum(grad * xhat)
+        early[7:8, :] += column_sum(grad)
         grad_mid = grad_out + norm_back(grad, gain_two, xhat, inverse)
         middle[rows] = grad_mid
         low = grad_mid.astype(BF)
         gm[rows] = low
-        small[10:11, :] += column_sum(low.astype(F32))
+        early[8:9, :] += column_sum(low.astype(F32))
 
     over_rows(result_rows)
     swap_ga.start()
@@ -789,94 +871,148 @@
     for i in range(4):
         sent_slab(attn, i)
 
+    stages = ((partner,), (along_z(1), along_z(2), along_z(3)), (along_x, along_y, across))
+    early_sums = (((early, early_got),), 12)
+    late_sums = (((late, late_got), (rel, rel_got)), 19)
+
+    def small_copies(sums, stage):
+        pairs, base = sums
+        first = (0, 1, 4)[stage]
+        for i, device in enumerate(stages[stage]):
+            for j, (src, got) in enumerate(pairs):
+                index = base + (first + i) * len(pairs) + j
+                yield src, got, first + i, remote(src, got.at[first + i], csend, crecv, index, device)
+
+    def small_start(sums, stage):
+        for _, _, _, copy in small_copies(sums, stage):
+            copy.start()
+
+    def small_finish(sums, stage):
+        copies = list(small_copies(sums, stage))
+        for _, _, _, copy in copies:
+            copy.wait()
+        for src, got, place, _ in copies:
+            src[...] += got[place]
+
+    def on_side(act_on):
+        for side in range(2):
+
+            @pl.when(r == side)
+            def _():
+                act_on(side)
+
+    def fill_early(side):
+        for s in range(4):
+            early[10 + s : 11 + s, side * half : (side + 1) * half] = bias_e[s]
+
+    on_side(fill_early)
+    early_store = pltpu.make_async_copy(early, early_out, local.at[9])
+    small_start(early_sums, 0)
+
     @pl.loop(0, 4)
     def _(n):
         s = slab_of(3 - n)
         g = slot(0, n)
-        attention_back_slab(
-            s, h1, gm, wq, wp, bias_q_of(s), rel_query, rel_back, codes, gqkv, back, bias_q, rel_acc, heads, half
-        )
+
+        def some_windows(first):
+            attention_back_slab(
+                s, first, h1, gm, wq, wp, bias_q_of(s), rel_query, rel_back, codes, gqkv, back, bias_q, rel_acc, heads, half
+            )
+
+        some_windows(0)
+
+        @pl.when(((n == 0) & is_end) | ((n == 2) & is_inner))
+        def _():
+            reduce_three(mlp, 3)
+
+        @pl.when((n > 1) & is_end)
+        def _():
+            reduce_three(attn, n - 2)
+
+        @pl.when(n == 3)
+        def _():
+            reduce_four(whole)
+
+        @pl.when(n == 0)
+        def _():
+            small_finish(early_sums, 0)
+            small_start(early_sums, 1)
+
+        some_windows(1)
+
+        @pl.when(n > 0)
+        def _():
+            reduce_two(attn, n - 1)
+
         for side in range(2):
             columns = slice(side * half, side * half + half)
             wq[g, side] = dot_tn(gqkv[...], h1[:, columns]).astype(BF).reshape(wq.shape[2:])
             wp[g, side] = dot_tn(attended[s], gm[:, columns]).astype(BF).reshape(wp.shape[2:])
         reduce_one(attn, n)
 
-        @pl.when(n == 0)
-        def _():
-            reduce_three(mlp, 3)
-
-        @pl.when(n > 0)
-        def _():
-            reduce_two(attn, n - 1)
-
-        @pl.when(n > 1)
-        def _():
-            reduce_three(attn, n - 2)
+        @pl.when((n == 3) & is_inner)
+        def _():
+            reduce_three(attn, 0)
+
+        @pl.when((n == 0) & is_inner)
+        def _():
+            reduce_three(mlp, 2)
 
     swap_gh1.start()
-    reduce_four((2,))
-    reduce_three(attn, 2)
-    reduce_two(attn, 3)
-    reduce_four((3,))
+    reduce_four(shrink)
     swap_gh1.wait()
 
     def input_rows(rows):
         value = tokens[rows].astype(F32)
         grad = (back[rows] + xr[rows]) * keep[rows]
         xhat, inverse = normalize(value)
-        small[6:7, :] += column_sum(grad * xhat)
-        small[7:8, :] += column_sum(grad)
+        late[0:1, :] += column_sum(grad * xhat)
+        late[1:2, :] += column_sum(grad)
         middle[rows] = middle[rows] + norm_back(grad, gain_one, xhat, inverse)
 
     over_rows(input_rows)
-    input_store = pltpu.make_async_copy(middle, input_grad, local.at[9])
+    input_store = pltpu.make_async_copy(middle, input_grad, local.at[10])
     input_store.start()
 
-    for s in range(4):
-        at = SMALL_ROWS - 8 + s
-        for side in range(2):
-
-            @pl.when(r == side)
-            def _():
-                small[at + 4 * side : at + 4 * side + 1, :half] = bias_e[s]
-                small[at + 4 * side : at + 4 * side + 1, half : half + bias_q.shape[2]] = bias_q[s]
-
-    rel[...] = rel_acc[:LANES] + rel_acc[LANES:]
-
-    def small_step(step, device):
-        first = remote(small, small_got.at[step], csend, crecv, 12 + 2 * step, device)
-        second = remote(rel, rel_got.at[step], csend, crecv, 13 + 2 * step, device)
-        first.start()
-        second.start()
-
-        def finish():
-            first.wait()
-            second.wait()
-            small[...] += small_got[step]
-            rel[...] += rel_got[step]
-
-        return finish
-
-    finish = small_step(0, partner)
+    def fill_late(side):
+        lanes = bias_q.shape[2]
+        for s in range(4):
+            late[2 + s : 3 + s, side * lanes : (side + 1) * lanes] = bias_q[s]
+
+    on_side(fill_late)
+    for part, at in ((0, 0), (1, COL_W)):
+        rows = slice(at, at + 32)
+        rel[part * 32 : part * 32 + 32] = rel_acc[rows] + rel_acc[LANES + at : LANES + at + 32]
+
+    small_start(late_sums, 0)
+
+    @pl.when(is_inner)
+    def _():
+        reduce_three(attn, 1)
+
+    reduce_three(attn, 2)
+    small_finish(late_sums, 0)
+    small_start(late_sums, 1)
+    reduce_five(whole)
+    reduce_two(attn, 3)
+    reduce_five(shrink)
+    small_finish(late_sums, 1)
+    small_start(late_sums, 2)
+    small_finish(early_sums, 1)
+    small_start(early_sums, 2)
     reduce_three(attn, 3)
-    finish()
-    finish = small_step(1, along_x)
     reduce_four(attn)
-    finish()
-    finish = small_step(2, along_y)
-    reduce_five(mlp)
-    finish()
-    finish = small_step(3, along_z(1))
+    small_finish(late_sums, 2)
+    small_finish(early_sums, 2)
+    early_store.start()
+    late_stores = [
+        pltpu.make_async_copy(late, late_out, local.at[6]),
+        pltpu.make_async_copy(rel, rel_out, local.at[7]),
+    ]
+    for copy in late_stores:
+        copy.start()
+    reduce_six(mlp)
     reduce_five(attn)
-    finish()
-    finish = small_step(4, along_z(2))
-    reduce_six(mlp)
-    finish()
-    small_store = pltpu.make_async_copy(small, small_out, local.at[6])
-    rel_store = pltpu.make_async_copy(rel, rel_out, local.at[7])
-    small_store.start()
-    rel_store.start()
     reduce_six(attn)
 
     swap_h1.wait_send()
@@ -891,12 +1027,11 @@
             for kind in range(4):
                 reduce_copy(a, n, kind).wait_send()
 
-            @pl.when(step_slab(a, n) != z)
-            def _():
-                reduce_copy(a, n, 4).wait_send()
-
-    small_store.wait()
-    rel_store.wait()
+            reduce_z(a, n, lambda copy: copy.wait_send())
+
+    for copy in late_stores:
+        copy.wait()
+    early_store.wait()
     result_store.wait()
     input_store.wait()
 
@@ -911,13 +1046,13 @@
     vmem_spec = pl.BlockSpec(memory_space=pltpu.VMEM)
     out_shape = [sds((own, width), BF), sds((own, width), F32)]
     out_shape += [sds(source.shape, BF) for source in sources]
-    out_shape += [sds((SMALL_ROWS, width), F32), sds((LANES, LANES), F32)]
+    out_shape += [sds((16, width), F32), sds((8, width), F32), sds((64, LANES), F32)]
     first, second = zip(*[halves(n) for n in rows])
     out_shape += [sds((4, 2, n, half), BF) for n in first]
     out_shape += [sds((4, 2, n, half), BF) for n in second]
     out_shape += [sds((4, n, half), BF) for n in second]
     out_shape += [sds((4, n, half), BF) for n in first]
-    out_shape += [sds((4, n, half), BF) for n in rows]
+    out_shape += [sds((6, n, half), BF) for n in rows]
     both = 2 * own
     vmem, dma = pltpu.VMEM, pltpu.SemaphoreType.DMA
     qkv_width = 2 * rows[0]
@@ -928,12 +1063,13 @@
     scratch += [vmem((own, width), F32)] * 3
     scratch += [vmem((max(both, 3 * rows[2]), half), BF), vmem((both, half), BF), vmem((both, qkv_width), BF)]
     scratch += [vmem((4, 2, first[2], half), BF)]
-    scratch += [vmem((4, 8, width), F32), vmem((SMALL_ROWS, width), F32), vmem((5, SMALL_ROWS, width), F32)]
-    scratch += [vmem((LANES, LANES), F32), vmem((5, LANES, LANES), F32)]
+    scratch += [vmem((4, 8, width), F32), vmem((16, width), F32), vmem((7, 16, width), F32)]
+    scratch += [vmem((8, width), F32), vmem((7, 8, width), F32)]
+    scratch += [vmem((64, LANES), F32), vmem((7, 64, LANES), F32)]
     scratch += [vmem((4, 1, half), F32), vmem((4, 1, qkv_width), F32), vmem((2 * LANES, LANES), F32)]
     scratch += [vmem((2 * LANES, LANES), BF), vmem((3 * LANES, LANES), BF), vmem((2, 32, HEAD), F32)]
-    scratch += [dma((4, 4, 6))] * 2 + [dma((4, 4, 5))] * 2 + [dma((4, 5))] * 2 + [dma((22,))] * 2
-    scratch += [dma((4,))] * 2 + [dma((8,))] * 2 + [dma((10,)), dma((4,))]
+    scratch += [dma((4, 4, 6))] * 2 + [dma((4, 4, 5)), dma((4, 4, 6))] + [dma((4, 5))] * 2 + [dma((33,))] * 2
+    scratch += [dma((4,))] * 2 + [dma((8,))] * 2 + [dma((11,)), dma((4,))]
     got = pl.pallas_call(
         kernel,
         out_shape=out_shape,
@@ -945,7 +1081,72 @@
         ),
         name="block_step",
     )(tokens, keep, out_grad, *vectors, qkv_bias, expand_bias, rel_height, rel_width, key_codes(), *sources)
-    return got[:8]
+    return got[:9]
+
+
+def finish_kernel(early, late, rel, *refs):
+    wide, (bias_q, bias_e, height, width_out, rms), rows_out = refs[:4], refs[4:9], refs[9:15]
+    outs, held, full, load, store = refs[15:19], refs[19:23], refs[23:27], refs[27], refs[28]
+    z = lax.axis_index("col")
+    loads = [pltpu.make_async_copy(src, to, load.at[i]) for i, (src, to) in enumerate(zip(wide, held))]
+    stores = [pltpu.make_async_copy(src, to, store.at[i]) for i, (src, to) in enumerate(zip(full, outs))]
+    for copy in loads:
+        copy.start()
+    places = ((late, 0), (late, 1), (early, 6), (early, 7), (early, 8), (early, 9))
+    for ref, (source, at) in zip(rows_out, places):
+        ref[...] = source[at, :]
+    features = early.shape[1]
+    scale = 1.0 / (early[5:6, 0:1] * features)
+    rms[...] = jnp.sqrt(jnp.sum(early[:8], axis=1, keepdims=True) * scale)
+    half = features // 2
+    part = bias_q.shape[1] // 2
+    bias_e[...] = early[pl.ds(10 + z, 1), :]
+    row = late[pl.ds(2 + z, 1), :]
+    for side in range(2):
+        for i in range(2):
+            at = (3 * side + 2 * i) * part
+            bias_q[i : i + 1, side * part : (side + 1) * part] = row[:, at : at + part]
+    count = height.shape[0]
+    turn = lax.broadcasted_iota(jnp.int32, (32, 32), 0) + lax.broadcasted_iota(jnp.int32, (32, 32), 1) == count - 1
+    turned = jnp.dot(turn.astype(F32), rel[:32], precision=lax.Precision.HIGHEST, preferred_element_type=F32)
+    height[...] = turned[:count, :HEAD]
+    width_out[...] = rel[32 : 32 + count, :HEAD]
+    for i in range(4):
+        loads[i].wait()
+        rows = held[i].shape[0]
+        step = rows // 5
+
+        @pl.loop(0, 5)
+        def _(m):
+            at = pl.ds(pl.multiple_of(m * step, step), step)
+            full[i][at] = held[i][at].astype(F32)
+
+        stores[i].start()
+    for copy in stores:
+        copy.wait()
+
+
+def finish_outputs(got, part):
+    early, late, rel = got[6:9]
+    grads = [value.reshape(-1, value.shape[-1]) for value in got[2:6]]
+    width = early.shape[1]
+    sds = jax.ShapeDtypeStruct
+    any_spec = pl.BlockSpec(memory_space=pl.ANY)
+    vmem_spec = pl.BlockSpec(memory_space=pltpu.VMEM)
+    out_shape = [sds((2, 2 * part), F32), sds((1, width), F32), sds((2 * SIDE - 1, HEAD), F32)]
+    out_shape += [sds((2 * SIDE - 1, HEAD), F32), sds((8, 1), F32)] + [sds((width,), F32)] * 6
+    out_shape += [sds(value.shape, F32) for value in grads]
+    return pl.pallas_call(
+        finish_kernel,
+        out_shape=out_shape,
+        in_specs=[vmem_spec] * 3 + [any_spec] * 4,
+        out_specs=[vmem_spec] * 11 + [any_spec] * 4,
+        scratch_shapes=[pltpu.VMEM(value.shape, BF) for value in grads]
+        + [pltpu.VMEM(value.shape, F32) for value in grads]
+        + [pltpu.SemaphoreType.DMA((4,))] * 2,
+        compiler_params=pltpu.CompilerParams(vmem_limit_bytes=VMEM_LIMIT // 2),
+        name="finish",
+    )(early, late, rel, *grads)
 
 
 VMEM_LIMIT = 64 * 1024 * 1024 - 512 * 1024
@@ -981,36 +1182,28 @@
         padded(tokens), keep, padded(out_grad), vectors, qkv_bias, expand_bias, rel_height, rel_width,
         (qkv_src, proj_src, expand_src, shrink_src),
     )
-    block_low, grad, qkv_got, proj_got, expand_got, shrink_got, small, rel = got
-    qkv_sum = qkv_got.astype(F32).reshape(3, local_width, rows).transpose(2, 0, 1)
-    proj_sum = proj_got.astype(F32).reshape(proj_weight.shape)
-    expand_sum = expand_got.astype(F32).reshape(expand_weight.shape)
-    shrink_sum = shrink_got.astype(F32).reshape(shrink_weight.shape)
-    rms = jnp.sqrt(jnp.sum(small[:5], axis=1) / (small[5, 0] * width))
-    slabs = small[SMALL_ROWS - 8 :].reshape(2, 4, width)
-    mine = lax.dynamic_index_in_dim(slabs, lax.axis_index("col"), axis=1, keepdims=False)
-    expand_bias_sum = mine[:, :hidden].reshape(-1)
-    qkv_bias_sum = mine[:, hidden : hidden + 3 * part].reshape(2, 3, part)[:, 0::2].transpose(1, 0, 2).reshape(2, -1)
-    height_sum = rel[:count, :head][::-1]
-    width_sum = rel[COL_W : COL_W + count, :head]
+    outs = finish_outputs(got, part)
+    qkv_bias_sum, expand_bias_sum, height_sum, width_sum, rms = outs[:5]
+    gain_one, shift_one, gain_two, shift_two, proj_bias_sum, shrink_bias_sum = outs[5:11]
+    qkv_sum, proj_sum, expand_sum, shrink_sum = outs[11:]
     return (
-        cut(block_low),
-        cut(grad),
-        small[6],
-        small[7],
-        qkv_sum,
+        cut(got[0]),
+        cut(got[1]),
+        gain_one,
+        shift_one,
+        qkv_sum.reshape(3, local_width, rows).transpose(2, 0, 1),
         qkv_bias_sum,
         height_sum,
         width_sum,
-        proj_sum,
-        small[10],
-        small[8],
-        small[9],
-        expand_sum,
-        expand_bias_sum,
-        shrink_sum,
-        small[11],
-        rms,
+        proj_sum.reshape(proj_weight.shape),
+        proj_bias_sum,
+        gain_two,
+        shift_two,
+        expand_sum.reshape(expand_weight.shape),
+        expand_bias_sum.reshape(-1),
+        shrink_sum.reshape(shrink_weight.shape),
+        shrink_bias_sum,
+        rms[:5, 0],
     )
 
 

time: 405 us -> 379 us (0.936)
  Pallas kernels: 375 us -> 362 us
  other arithmetic: 9.64 us -> 1.3 us
  local copies, waits for them, and re-layouts: 17.8 us -> 13.7 us
    pallas_call x1, Pallas kernels: 375 us -> 356 us  [run_kernel(): pl.pallas_call(kernel, out_shape=out_shape, in_specs=[vmem_spec, vmem_spe...]
    reshape x3 -> x0, other arithmetic: 6.51 us -> none  [the longest x1 3.47 us: over_chips(): shrink_sum = shrink_got.astype(F32).reshape(shrink_weight.shape)]
    pallas_call x0 -> x1, Pallas kernels: none -> 5.91 us  [finish_outputs(): pl.pallas_call(finish_kernel, out_shape=out_shape, in_specs=[vmem_spec] *...]
    slice x7 -> x1, local copies, waits for them, and re-layouts: 5 us -> 0.63 us  [over_chips(): rms[:5, 0]]
where the time goes in v3:
time: 379 us; the launch traced here: 378 us
  Pallas kernels  362 us (96%)
  local copies, waits for them, and re-layouts  13.7 us (4%)
    pallas_call x1, Pallas kernels, run_kernel(): pl.pallas_call(kernel, out_shape=out_shape, in_specs=[vmem_spec, vmem_spe...  356 us
    slice x2, local copies, waits for them, and re-layouts, cut(): grid = value.reshape(windows, side, SIDE_PAD, -1)[:, :, :side]  7.97 us

profile of v3, /device:TPU:0, one launch (start us, length us, event | category | flops | bytes accessed | tf_op | source)
XLA Modules:
  0.0 377.8 jit_solution(16390862710566120930)
XLA Ops:
  0.7 0.7 convert_element_type.8
  1.3 0.1 reshape.96
  1.4 0.8 reshape.114.keep
  2.3 1.3 copy.39
  3.6 0.0 copy-start.7
  3.6 1.1 pad.11
  4.7 0.5 copy-done.7
  5.2 0.1 copy.40
  5.4 1.1 pad.13
  6.5 356.1 %block_step.1 = (bf16[448,1280]{1,0:T(8,128)(2,1)}, f32[448,1280]{1,0:T(8,128)}, bf16[3,2,160,640]{3,2,1,0:T(8,128)(2,1)}, bf16[2,2,80,640]{3,2,1,0:T(8,128)(2,1...) custom-call(bf16[448,1280]{1,0:T(8,128)(2,1)} %bitcast.29, ...), custom_call_target="tpu_custom_call" | custom-call | tf_op jit(solution)/shard_map/block_step/pallas_call | solution.py:1073
  362.6 0.0 copy-start.2
  362.6 3.3 copy.42
  365.9 0.0 copy-start
  365.9 0.0 copy-start.1
  365.9 0.0 copy-start.3
  365.9 0.0 copy-start.4
  365.9 0.0 copy-start.5
  366.0 0.0 copy-start.6
  366.0 4.6 %copy.43 = f32[2,14,14,1280]{3,0,2,1:T(2,128)} copy(f32[2,14,14,1280]{3,2,1,0:T(8,128)} %bitcast.31) | data formatting | bytes 4014080 | tf_op jit(solution)/shard_map/slice | solution.py:1169
  370.6 0.0 copy-done.2
  370.6 0.0 copy-done
  370.6 0.0 copy-done.1
  370.6 0.0 copy-done.3
  370.6 0.0 copy-done.4
  370.6 0.0 copy-done.5
  370.6 0.0 copy-done.6
  370.7 5.9 %finish.1 = (f32[2,320]{1,0:T(2,128)}, f32[1,1280]{1,0:T(1,128)S(1)}, f32[27,80]{1,0:T(8,128)}, f32[27,80]{1,0:T(8,128)}, f32[8,1]{1,0:T(8,128)S(1)}, /*index=5*...) custom-call(f32[16,1280]{1,0:T(8,128)S(1)} %copy-done.4, ...), custom_call_target="tpu_custom_call" | custom-call | tf_op jit(solution)/shard_map/finish/pallas_call | solution.py:1139
  376.6 0.6 slice_reduce_fusion
  377.2 0.6 reduce
  (1 shorter events, 0.0 us)
Async XLA Ops:
  3.6 1.6 copy-start.7
  362.6 8.0 %copy-start.2 = (bf16[3,2,160,640]{3,2,1,0:T(8,128)(2,1)S(1)}, bf16[3,2,160,640]{3,2,1,0:T(8,128)(2,1)}, u32[]{:S(2)}) copy-start(bf16[3,2,160,640]{3,2,1,0:T(8,128)(2,1)} %get-tuple-element.46) | copy-start | bytes 3686404
  365.9 4.7 %copy-start = (bf16[2,320,1280]{2,1,0:T(8,128)(2,1)S(1)}, bf16[2,320,1280]{2,1,0:T(8,128)(2,1)}, u32[]{:S(2)}) copy-start(bf16[2,320,1280]{2,1,0:T(8,128)(2,1)} %get-tuple-element.48) | copy-start | bytes 4915204
  365.9 4.7 %copy-start.1 = (bf16[2,2,320,640]{3,2,1,0:T(8,128)(2,1)S(1)}, bf16[2,2,320,640]{3,2,1,0:T(8,128)(2,1)}, u32[]{:S(2)}) copy-start(bf16[2,2,320,640]{3,2,1,0:T(8,128)(2,1)} %get-tuple-element.49) | copy-start | bytes 4915204
  365.9 4.7 %copy-start.3 = (bf16[2,2,80,640]{3,2,1,0:T(8,128)(2,1)S(1)}, bf16[2,2,80,640]{3,2,1,0:T(8,128)(2,1)}, u32[]{:S(2)}) copy-start(bf16[2,2,80,640]{3,2,1,0:T(8,128)(2,1)} %get-tuple-element.47) | copy-start | bytes 1228804
  365.9 4.7 %copy-start.4 = (f32[16,1280]{1,0:T(8,128)S(1)}, f32[16,1280]{1,0:T(8,128)}, u32[]{:S(2)}) copy-start(f32[16,1280]{1,0:T(8,128)} %get-tuple-element.43.early) | copy-start | bytes 245764
  365.9 4.7 %copy-start.5 = (f32[8,1280]{1,0:T(8,128)S(1)}, f32[8,1280]{1,0:T(8,128)}, u32[]{:S(2)}) copy-start(f32[8,1280]{1,0:T(8,128)} %get-tuple-element.44.late) | copy-start | bytes 122884
  366.0 4.7 %copy-start.6 = (f32[64,128]{1,0:T(8,128)S(1)}, f32[64,128]{1,0:T(8,128)}, u32[]{:S(2)}) copy-start(f32[64,128]{1,0:T(8,128)} %get-tuple-element.45.rel) | copy-start | bytes 98308
